TPU v7x, 128 devices: a whole 4x4x4 slice. The times are simulated.
128 devices in a mesh: ctx: 8 (over y, z_lo), tp: 16 (over x, z_hi, core).
Axes of the slice: x: 4, y: 4, z: 4 (z_hi: 2, z_lo: 2; z = z_hi * 2 + z_lo), core: 2. Of those that a mesh axis runs over, the one named last changes fastest.
Arguments:
- context: bfloat16 [16384, 4096], P('ctx', 'tp'), may hold values from -6 to 6
- residual: bfloat16 [16384, 2048], P(('ctx', 'tp')), may hold values from -6 to 6
- o_weight: bfloat16 [4096, 2048], P('tp'), may hold values from -0.09375 to 0.09375
- norm_gain: bfloat16 [2048], replicated, may hold values from 0.099609375 to 1.8984375
- routes: int32 [16384, 4], P(('ctx', 'tp')), may hold values from 0 to 127, all different within a row; in each aligned block of 128 rows (0 to 127, 128 to 255, ...) at most 6 rows name the same one
- gate_weights: float32 [16384, 4], P(('ctx', 'tp')), may hold values from 0.05 to 0.5
- expert_in: bfloat16 [128, 2048, 1536], P(('ctx', 'tp')), may hold values from -0.125 to 0.125
- expert_out: bfloat16 [128, 768, 2048], P(('ctx', 'tp')), may hold values from -0.21875 to 0.21875
- cotangent: bfloat16 [16384, 2048], P(('ctx', 'tp')), may hold values from -6 to 6
Outputs:
- layer_out: bfloat16 [16384, 2048], P(('ctx', 'tp'))
- d_context: bfloat16 [16384, 4096], P('ctx', 'tp')
- d_residual: bfloat16 [16384, 2048], P(('ctx', 'tp'))
- d_o_weight: float32 [4096, 2048], P('tp', 'ctx')
- d_gain: float32 [2048], replicated
- d_expert_in: bfloat16 [128, 2048, 1536], P(('ctx', 'tp'))
- d_expert_out: bfloat16 [128, 768, 2048], P(('ctx', 'tp'))
Inputs may be any that keep to these rules, and one draw needn't show every extreme that they name: `routes`: each token names 4 different experts; the 128 tokens of one device (aligned blocks) name one expert at most 6 times, a bound that some block reaches.
All inputs are finite; a program needn't handle non-finite values.
Results may differ from a plain program's by a relative error of at most 0.019.
Values may be sent and summed in bfloat16 or wider, within the bound.
No kernel may reach another device: no remote copies, remote signals or barrier semaphores. Data moves between devices by JAX's collectives and lax.ppermute only.
A program may use at most 128 MiB of HBM per device.

v0:
```python
import functools

import jax
import jax.numpy as jnp
from jax import lax
from jax.experimental import pallas as pl
from jax.experimental.pallas import tpu as pltpu
from jax.sharding import PartitionSpec as P

BF = jnp.bfloat16
F32 = jnp.float32
SLOTS = 6
GROUP = 8
PACK = 3
MIB = 1024 * 1024
BIG = ("expert", "expert_y", "weight_give", "weight_own", "context_grad")


def mm(a, b, da=1, db=0):
    return lax.dot_general(a, b, (((da,), (db,)), ((), ())), preferred_element_type=F32)


def contract(left_arr, right_arr, left_dim, right_dim):
    return mm(left_arr, right_arr, left_dim, right_dim)


def iota(shape, dim):
    return lax.broadcasted_iota(jnp.int32, shape, dim)


def call(body, name, out, grid, in_specs, out_specs, scratch=(), flops=0, nbytes=0):
    return pl.pallas_call(
        body,
        out_shape=out,
        grid_spec=pltpu.PrefetchScalarGridSpec(
            num_scalar_prefetch=0,
            grid=grid,
            in_specs=in_specs,
            out_specs=out_specs,
            scratch_shapes=scratch,
        ),
        compiler_params=pltpu.CompilerParams(
            dimension_semantics=("arbitrary",) * len(grid), vmem_limit_bytes=(56 if name in BIG else 26) * MIB
        ),
        cost_estimate=pl.CostEstimate(flops=flops, bytes_accessed=nbytes, transcendentals=0),
        name=name,
    )


def whole(shape):
    n = len(shape)
    return pl.BlockSpec(shape, lambda i: (0,) * n)


def sds(shape, dtype):
    return jax.ShapeDtypeStruct(shape, dtype)


def slot_table(routes, n_exp):
    rows = routes.shape[0]
    lane = iota((rows, n_exp), 1)
    named = jnp.zeros((rows, n_exp), F32)
    for k in range(routes.shape[1]):
        named = named + (routes[:, k : k + 1] == lane).astype(F32)
    before = (iota((rows, rows), 0) > iota((rows, rows), 1)).astype(BF)
    rank = mm(before, named.astype(BF))
    return jnp.where(named > 0, rank, -1.0)


def gate_table(routes, gates, n_exp):
    rows = routes.shape[0]
    lane = iota((rows, n_exp), 1)
    table = jnp.zeros((rows, n_exp), F32)
    for k in range(routes.shape[1]):
        table = table + jnp.where(routes[:, k : k + 1] == lane, gates[:, k : k + 1], 0.0)
    return table


def thirds(values):
    high = values.astype(BF)
    rest = values - high.astype(F32)
    middle = rest.astype(BF)
    low = (rest - middle.astype(F32)).astype(BF)
    return high, middle, low


def pick_rows(slot, first, count):
    rows, n_exp = slot.shape
    row = iota((count, n_exp), 0) + first
    spread = (row // GROUP == iota((count, n_exp), 1)).astype(BF)
    at = mm(spread, slot.astype(BF), 1, 1)
    place = (iota((count, rows), 0) % GROUP).astype(F32)
    main = (at == place) & (place < SLOTS)
    tails = [(at == (place - SLOTS) * PACK + c) & (place >= SLOTS) for c in range(PACK)]
    return spread, main, tails


def pack_tokens(values, main, tails, quarter):
    out = []
    last = values[:, PACK * quarter :]
    for c in range(PACK):
        pick = jnp.concatenate([main.astype(BF), tails[c].astype(BF)], axis=1)
        source = jnp.concatenate([values[:, c * quarter : (c + 1) * quarter], last], axis=0)
        out.append(mm(pick, source))
    return out


def block_perm(count):
    real = count * SLOTS // GROUP
    row, col = iota((real, count), 0), iota((real, count), 1)
    owner, slot = row // SLOTS, row % SLOTS
    same = owner == col // GROUP
    place = col % GROUP
    main = same & (place == slot)
    tails = [
        same & (place == SLOTS + slot // PACK) & (slot % PACK == c) for c in range(PACK)
    ]
    return main.astype(BF), [t.astype(BF) for t in tails]


def block_perm_back(count):
    real = count * SLOTS // GROUP
    row, col = iota((count, real), 0), iota((count, real), 1)
    place, slot = row % GROUP, col % SLOTS
    same = row // GROUP == col // SLOTS
    main = same & (place == slot)
    tails = [
        same & (place == SLOTS + slot // PACK) & (slot % PACK == c) for c in range(PACK)
    ]
    return [jnp.concatenate([main.astype(BF), t.astype(BF)], axis=1) for t in tails]


def unpack(packed, perm, quarter):
    main, tails = perm
    head = mm(main, packed).astype(BF)
    stack = jnp.concatenate([packed[:, c * quarter : (c + 1) * quarter] for c in range(PACK)], axis=0)
    tail = mm(jnp.concatenate(tails, axis=1), stack).astype(BF)
    return jnp.concatenate([head, tail], axis=1)


def repack(rows, perm, quarter):
    last = rows[:, PACK * quarter :]
    out = []
    for c in range(PACK):
        source = jnp.concatenate([rows[:, c * quarter : (c + 1) * quarter], last], axis=0)
        out.append(mm(perm[c], source).astype(BF))
    return jnp.concatenate(out, axis=1)


def pack_grads_body(n_exp, rows, routes, gates, cot, out, slot, high, middle, low):
    i = pl.program_id(0)

    @pl.when(i == 0)
    def _():
        slot[...] = slot_table(routes[...], n_exp)
        high[...], middle[...], low[...] = thirds(gate_table(routes[...], gates[...], n_exp))

    quarter = cot.shape[1] // 4
    spread, main, tails = pick_rows(slot[...], i * rows, rows)
    gate = (mm(spread, high[...], 1, 1) + mm(spread, middle[...], 1, 1)) + mm(spread, low[...], 1, 1)
    parts = pack_tokens(cot[...], main, tails, quarter)
    for c in range(PACK):
        own = jnp.sum(jnp.where(main | tails[c], gate, 0.0), axis=1, keepdims=True)
        out[:, c * quarter : (c + 1) * quarter] = (parts[c] * own).astype(BF)


def pack_grads(routes, gates, cot, n_exp):
    tok, width = cot.shape
    total, steps = n_exp * GROUP, 4
    rows = total // steps
    table = pltpu.VMEM((tok, n_exp), BF)
    return call(
        functools.partial(pack_grads_body, n_exp, rows),
        "pack_grads",
        sds((total, width * 3 // 4), BF),
        (steps,),
        [whole(routes.shape), whole(gates.shape), whole(cot.shape)],
        pl.BlockSpec((rows, width * 3 // 4), lambda i: (i, 0)),
        [pltpu.VMEM((tok, n_exp), F32), table, table, table],
        flops=2 * total * 2 * tok * width,
        nbytes=8 * total * width,
    )(routes, gates, cot)


def norm_pack_body(n_exp, rows, routes, keep_a, keep_b, *refs):
    got_a, got_b, residual, gain, packed_g, out, mixed_out, slot, normed_h = (
        refs[:3], refs[3], *refs[4:]
    )
    i = pl.program_id(0)

    @pl.when(i == 0)
    def _():
        slot[...] = slot_table(routes[...], n_exp)
        tok, width = residual.shape
        step = 32

        def norm(j, carry):
            at = pl.ds(pl.multiple_of(j * step, step), step)
            left = keep_a[at, :]
            for part in got_a:
                left = left + part[at, :].astype(F32)
            right = keep_b[at, :] + got_b[at, :].astype(F32)
            total = jnp.concatenate([left, right], axis=1)
            mixed = (residual[at, :].astype(F32) + total).astype(BF)
            mixed_out[at, :] = mixed
            mixed = mixed.astype(F32)
            inv_rms = lax.rsqrt(jnp.mean(mixed * mixed, axis=-1, keepdims=True) + 1e-06)
            normed_h[at, :] = (mixed * inv_rms * gain[...].astype(F32)).astype(BF)
            return carry

        lax.fori_loop(0, tok // step, norm, 0)

    quarter = residual.shape[1] // 4
    _, main, tails = pick_rows(slot[...], i * rows, rows)
    packed = pack_tokens(normed_h[...], main, tails, quarter)
    for c in range(PACK):
        out[:, c * quarter : (c + 1) * quarter] = packed[c].astype(BF)
    out[:, PACK * quarter :] = packed_g[...]


def norm_pack(routes, keep_a, keep_b, got_a, got_b, residual, gain, packed_g, n_exp):
    tok, width = residual.shape
    total, steps = n_exp * GROUP, 4
    rows = total // steps
    args = (routes, keep_a, keep_b, *got_a, got_b, residual, gain)
    return call(
        functools.partial(norm_pack_body, n_exp, rows),
        "norm_pack",
        (sds((total, width * 3 // 2), BF), sds((tok, width), BF)),
        (steps,),
        [whole(a.shape) for a in args] + [pl.BlockSpec((rows, width * 3 // 4), lambda i: (i, 0))],
        (pl.BlockSpec((rows, width * 3 // 2), lambda i: (i, 0)), whole((tok, width))),
        [pltpu.VMEM((tok, n_exp), F32), pltpu.VMEM((tok, width), BF)],
        flops=2 * total * 2 * tok * width,
        nbytes=8 * total * width,
    )(*args, packed_g)


def pick_tokens(slot):
    rows, n_exp = slot.shape
    total = n_exp * GROUP
    spread = (iota((n_exp, total), 1) // GROUP == iota((n_exp, total), 0)).astype(BF)
    at = mm(slot.astype(BF), spread)
    place = (iota((rows, total), 1) % GROUP).astype(F32)
    main = (at == place) & (place < SLOTS)
    tails = [(at == (place - SLOTS) * PACK + c) & (place >= SLOTS) for c in range(PACK)]
    return spread, main, tails


def combine_grads_body(n_exp, routes, packed, mixed_ref, gain, cot, out, res_out):
    tok, width = cot.shape
    quarter = width // 4
    _, main, tails = pick_tokens(slot_table(routes[...], n_exp))
    heads, last = [], jnp.zeros((tok, quarter), F32)
    for c in range(PACK):
        pick = jnp.concatenate([main.astype(BF), tails[c].astype(BF)], axis=0)
        both = mm(pick, packed[:, c * quarter : (c + 1) * quarter])
        heads.append(both[:tok])
        last = last + both[tok:]
    grad_h = jnp.concatenate(heads + [last], axis=1)
    mixed = mixed_ref[...].astype(F32)
    inv_rms = lax.rsqrt(jnp.mean(mixed * mixed, axis=-1, keepdims=True) + 1e-06)
    normed = mixed * inv_rms
    d_gain = jnp.sum(grad_h * normed, axis=0, keepdims=True)
    high, middle, low = thirds(d_gain)
    row = iota((16, width), 0)
    gain_rows = jnp.where(row == 0, high.astype(F32), 0.0)
    gain_rows = jnp.where(row == 1, middle.astype(F32), gain_rows)
    gain_rows = jnp.where(row == 2, low.astype(F32), gain_rows)
    grad_n = grad_h * gain[...].astype(F32)
    inner = jnp.mean(grad_n * normed, axis=-1, keepdims=True)
    d_res = cot[...].astype(F32) + inv_rms * (grad_n - normed * inner)
    d_res = d_res.astype(BF)
    gain_rows = gain_rows.astype(BF)
    res_out[...] = d_res
    out[0:tok, :] = d_res
    out[tok : tok + 16, :] = gain_rows


def combine_grads(routes, packed, mixed, gain, cot, n_exp):
    tok, width = cot.shape
    return call(
        functools.partial(combine_grads_body, n_exp),
        "combine_grads",
        (sds((tok + 16, width), BF), sds((tok, width), BF)),
        (1,),
        [whole(a.shape) for a in (routes, packed, mixed, gain, cot)],
        (whole((tok + 16, width)), whole((tok, width))),
        flops=2 * packed.shape[0] * 2 * tok * width,
        nbytes=8 * packed.shape[0] * width,
    )(routes, packed, mixed, gain, cot)


def combine_out_body(n_exp, routes, gates, packed, mixed, out):
    tok, width = mixed.shape
    quarter = width // 4
    spread, main, tails = pick_tokens(slot_table(routes[...], n_exp))
    parts = thirds(gate_table(routes[...], gates[...], n_exp))
    gate = (mm(parts[0], spread) + mm(parts[1], spread)) + mm(parts[2], spread)
    high = gate.astype(BF)
    low = (gate - high.astype(F32)).astype(BF)
    none = jnp.zeros_like(high)
    last = jnp.zeros((tok, quarter), F32)
    for c in range(PACK):
        pick = jnp.concatenate(
            [
                jnp.where(main, high, none),
                jnp.where(main, low, none),
                jnp.where(tails[c], high, none),
                jnp.where(tails[c], low, none),
            ],
            axis=0,
        )
        both = mm(pick, packed[:, c * quarter : (c + 1) * quarter])
        at = slice(c * quarter, (c + 1) * quarter)
        head = both[:tok] + both[tok : 2 * tok]
        out[:, at] = (mixed[:, at].astype(F32) + head).astype(BF)
        last = last + (both[2 * tok : 3 * tok] + both[3 * tok :])
    at = slice(PACK * quarter, width)
    out[:, at] = (mixed[:, at].astype(F32) + last).astype(BF)


def combine_out(routes, gates, packed, mixed, n_exp):
    tok, width = mixed.shape
    return call(
        functools.partial(combine_out_body, n_exp),
        "combine_out",
        sds((tok, width), BF),
        (1,),
        [whole(a.shape) for a in (routes, gates, packed, mixed)],
        whole((tok, width)),
        flops=2 * packed.shape[0] * 4 * tok * width,
        nbytes=6 * packed.shape[0] * width,
    )(routes, gates, packed, mixed)


SUB = 256


def unpack_rows(packed, quarter):
    perm = block_perm(SUB)
    return jnp.concatenate(
        [
            unpack(packed[j * SUB : (j + 1) * SUB, :], perm, quarter)
            for j in range(packed.shape[0] // SUB)
        ],
        axis=0,
    )


def repack_rows(rows, out, quarter):
    perm = block_perm_back(SUB)
    real = SUB * SLOTS // GROUP
    for j in range(rows.shape[0] // real):
        out[j * SUB : (j + 1) * SUB, :] = repack(rows[j * real : (j + 1) * real, :], perm, quarter)


def expert_body(
    packed_h, packed_g, weight_in, weight_out, rows_out, grads_out, act_out, ggu_out, packed_out
):
    width, both = weight_in.shape
    hidden = both // 2
    quarter = width // 4
    rows = unpack_rows(packed_h, quarter)
    rows_out[...] = rows
    gate_part = mm(rows, weight_in[:, :hidden])
    up_part = mm(rows, weight_in[:, hidden:])
    sigma = jax.nn.sigmoid(gate_part)
    silu = gate_part * sigma
    act_out[...] = (silu * up_part).astype(BF)
    grads = unpack_rows(packed_g, quarter)
    grads_out[...] = grads
    grad_act = mm(grads, weight_out[...], 1, 1)
    grad_gate = (grad_act * up_part * sigma * (1.0 + gate_part * (1.0 - sigma))).astype(BF)
    grad_up = (grad_act * silu).astype(BF)
    ggu_out[:, :hidden] = grad_gate
    ggu_out[:, hidden:] = grad_up
    back = mm(jnp.concatenate([grad_gate, grad_up], axis=1), weight_in[...], 1, 1).astype(BF)
    repack_rows(back, packed_out, quarter)


def once(shape):
    n = len(shape)
    return pl.BlockSpec(shape, lambda i: (0,) * n, pipeline_mode=pl.Buffered(buffer_count=1))


def expert_call(packed, weight_in, weight_out):
    width, both = weight_in.shape
    hidden = both // 2
    steps = 2
    block = packed.shape[0] // steps
    real = block * SLOTS // GROUP
    part = packed.shape[1] // 2
    at = lambda i: (i, 0)
    return call(
        expert_body,
        "expert",
        (
            sds((real * steps, width), BF),
            sds((real * steps, width), BF),
            sds((real * steps, hidden), BF),
            sds((real * steps, both), BF),
            sds((packed.shape[0], part), BF),
        ),
        (steps,),
        [
            pl.BlockSpec((block, part), at),
            pl.BlockSpec((block, part), lambda i: (i, 1)),
            once(weight_in.shape),
            once(weight_out.shape),
        ],
        (
            pl.BlockSpec((real, width), at),
            pl.BlockSpec((real, width), at),
            pl.BlockSpec((real, hidden), at),
            pl.BlockSpec((real, both), at),
            pl.BlockSpec((block, part), at),
        ),
        flops=5 * real * steps * both * width,
        nbytes=2 * both * width + 10 * real * steps * width,
    )(packed, packed, weight_in, weight_out)


def expert_y_body(act, weight_out, packed_out):
    rows = mm(act[...], weight_out[...]).astype(BF)
    repack_rows(rows, packed_out, weight_out.shape[1] // 4)


def expert_y_call(act, weight_out):
    hidden, width = weight_out.shape
    steps = 2
    real = act.shape[0] // steps
    block = real * GROUP // SLOTS
    at = lambda i: (i, 0)
    return call(
        expert_y_body,
        "expert_y",
        sds((block * steps, width * 3 // 4), BF),
        (steps,),
        [pl.BlockSpec((real, hidden), at), whole(weight_out.shape)],
        pl.BlockSpec((block, width * 3 // 4), at),
        flops=2 * real * steps * hidden * width,
        nbytes=2 * hidden * width + 4 * real * steps * width,
    )(act, weight_out)


def rows_of(ref, order, places):
    return jnp.concatenate([ref[order[p]] for p in places], axis=0)


def product(order, places, ctx_own, ctx_got, w_own, w_got, cols):
    own = mm(rows_of(ctx_own, order, places), w_own[:, cols])
    return own + mm(rows_of(ctx_got, order, places), w_got[:, cols])


def halves(w):
    half = w.shape[1] // 2
    return slice(0, half), slice(half, 2 * half)


def project_first_body(order, ctx_own, ctx_got, w_own, w_got, over_z, *over_x):
    left, right = halves(w_own)
    args = (ctx_own, ctx_got, w_own, w_got)
    over_z[...] = product(order, [1, 3, 5, 7], *args, left).astype(BF)
    for d in range(3):
        over_x[d][...] = product(order, [2 * d + 2, 2 * d + 3], *args, right).astype(BF)


def project_keep_body(order, ctx_own, ctx_got, w_own, w_got, keep_a, keep_b):
    left, right = halves(w_own)
    args = (ctx_own, ctx_got, w_own, w_got)
    keep_b[...] = product(order, [0, 1], *args, right)
    keep_a[...] = product(order, [0, 2, 4, 6], *args, left)


def add_body(order, kept_a, kept_b, got_z, got_1, got_2, got_3, keep_a, keep_b, over_z, *over_x):
    tok = keep_a.shape[0]
    keep_a[...] = kept_a[0:tok, :] + got_z[0:tok, :].astype(F32)
    for d in range(3):
        at = slice((d + 1) * tok, (d + 2) * tok)
        over_x[d][...] = (kept_a[at, :] + got_z[at, :].astype(F32)).astype(BF)
    total = kept_b[...]
    for got in (got_1, got_2, got_3):
        total = total + got[...].astype(F32)
    keep_b[...] = total[:tok]
    over_z[...] = total[tok:].astype(BF)


def plain(body, name, outs, order, *args, flops=0, scratch=()):
    nbytes = sum(a.size * a.dtype.itemsize for a in args)
    nbytes += sum(o.size * o.dtype.itemsize for o in outs)
    return call(
        body,
        name,
        tuple(outs),
        (1,),
        [pl.BlockSpec(memory_space=pltpu.SMEM)] + [whole(a.shape) for a in args],
        tuple(whole(o.shape) for o in outs),
        scratch,
        flops=flops,
        nbytes=nbytes,
    )(order, *args)


N_BLOCKS = 11


def gather_parts(blocks, first, last):
    same_z, other_z, left_z, right_z = blocks[:4], blocks[4], blocks[5:8], blocks[8:]
    cut = left_z[0].shape[1]
    left, right = [], []
    for d in range(4):
        left += [same_z[d][first:last, :cut]]
        left += [left_z[d - 1][first:last, :] if d else other_z[first:last, :cut]]
        right += [same_z[d][first:last, cut:]]
        right += [right_z[d - 1][first:last, :] if d else other_z[first:last, cut:]]
    return left, right


def gather_rows(blocks):
    left, right = gather_parts(blocks, 0, blocks[0].shape[0] - 16)
    return jnp.concatenate(left, axis=0), jnp.concatenate(right, axis=0)


def weight_give_body(order, ctx_got, *refs):
    blocks, (give, gain_out) = refs[:N_BLOCKS], refs[N_BLOCKS:]
    tok = ctx_got.shape[1]
    ctx = rows_of(ctx_got, order, range(8))
    gains = gather_parts(blocks, tok, tok + 16)
    first = 0
    for h, rows in enumerate(gather_rows(blocks)):
        last = first + rows.shape[1]
        give[:, first:last] = mm(ctx, rows, 0, 0).astype(BF)
        total = jnp.zeros((16, last - first), F32)
        for part in gains[h]:
            total = total + part.astype(F32)
        total = jnp.sum(total, axis=0, keepdims=True)
        gain_out[:, first:last] = jnp.broadcast_to(total, (8, last - first))
        first = last


def context_grad_body(order, w_own, w_got, *refs):
    blocks, (own, give) = refs[:N_BLOCKS], refs[N_BLOCKS:]
    tok = own.shape[1]
    left, right = gather_rows(blocks)
    cut = left.shape[1]
    for w, out in ((w_got, give), (w_own, own)):
        grad = mm(left, w[:, :cut], 1, 1) + mm(right, w[:, cut:], 1, 1)
        grad = grad.astype(BF)
        for p in range(8):
            out[order[p] // 2] = grad[p * tok : (p + 1) * tok]


def weight_own_body(order, ctx_own, got, gain_own, gain_got, *refs):
    blocks, outs, held = refs[:N_BLOCKS], refs[N_BLOCKS:-1], refs[-1]
    cols = ctx_own.shape[2]
    n_ctx, _, width = held.shape
    ctx = rows_of(ctx_own, order, range(8))
    parts = thirds(gain_own[0:1, :] + gain_got[0:1, :])
    row = iota((32, width), 0)
    gain = jnp.zeros((32, width), F32)
    for p in range(3):
        for j in range(n_ctx):
            piece = parts[p][:, j * width : (j + 1) * width].astype(F32)
            gain = jnp.where(row == p * n_ctx + j, piece, gain)
    gain = gain.astype(BF)
    first = 0
    for rows in gather_rows(blocks):
        last = first + rows.shape[1]
        grad = mm(ctx, rows, 0, 0) + got[:, first:last].astype(F32)
        grad = grad.astype(BF)
        for j in range(first // width, last // width):
            held[j, 0:cols, :] = grad[:, j * width - first : (j + 1) * width - first]
            held[j, cols : cols + 32, :] = gain
        first = last
    y, z = order[8] // 2, order[8] % 2
    for d, out in enumerate(outs):
        for o in range(2):
            out[o] = held[(y + d) % (n_ctx // 2) * 2 + (z + o) % 2]


def trade(values):
    n_all = lax.axis_size("ctx") * lax.axis_size("tp")
    shaped = values.reshape(n_all, GROUP, values.shape[1])
    moved = lax.all_to_all(shaped, ("ctx", "tp"), split_axis=0, concat_axis=0, tiled=True)
    return moved.reshape(values.shape)


def on_device(
    context, residual, o_weight, norm_gain, routes, gate_weights, expert_in, expert_out, cotangent
):
    tok, width = residual.shape
    n_tp = lax.axis_size("tp")
    n_ctx = lax.axis_size("ctx")
    n_exp = n_tp * n_ctx
    chips = n_tp // 2
    cols = context.shape[1]
    core = lax.axis_index("tp") % 2
    gain_row = norm_gain.reshape(1, width)

    t = lax.axis_index("tp")
    x, z = t // 4, t // 2 % 2
    pairs = [(d, o) for d in range(4) for o in range(2)]
    order = jnp.stack([(x + d) % 4 * 4 + (z ^ o) * 2 + core for d, o in pairs])
    came = jnp.stack([(x - d) % 4 * 4 + (z ^ o) * 2 + core for d, o in pairs])

    def over_x(d):
        return [(u, (u + 4 * d) % n_tp) for u in range(n_tp)]

    over_z = [(u, u ^ 2) for u in range(n_tp)]
    swap = [(u, u ^ 1) for u in range(n_tp)]

    def move(values, perm):
        return lax.ppermute(values, "tp", perm)

    ctx_own = context.reshape(n_tp, tok, cols)
    ctx_got = move(ctx_own, swap)
    w_got = move(o_weight, swap)
    packed_g = pack_grads(routes, gate_weights, cotangent, n_exp)
    half = width // 2
    operands = (ctx_own, ctx_got, o_weight, w_got)
    per_block = 4 * tok * cols * half
    send_z, *send_x = plain(
        project_first_body,
        "project_first",
        [sds((4 * tok, half), BF)] + [sds((2 * tok, half), BF)] * 3,
        order,
        *operands,
        flops=10 * per_block,
    )
    got_z = move(send_z, over_z)
    got_x = [move(send_x[d], over_x(d + 1)) for d in range(3)]
    kept_a, kept_b = plain(
        project_keep_body,
        "project_keep",
        [sds((4 * tok, half), F32), sds((2 * tok, half), F32)],
        order,
        *operands,
        flops=6 * per_block,
    )
    keep_a, keep_b, send_b, *send_a = plain(
        add_body,
        "add",
        [sds((tok, half), F32)] * 2 + [sds((tok, half), BF)] * 4,
        order,
        kept_a,
        kept_b,
        got_z,
        *got_x,
    )
    got_a = [move(send_a[d], over_x(d + 1)) for d in range(3)]
    got_b = move(send_b, over_z)

    packed_h, mixed = norm_pack(
        routes, keep_a, keep_b, got_a, got_b, residual, gain_row, packed_g, n_exp
    )
    rows_in = trade(packed_h)

    weight_in, weight_out = expert_in[0], expert_out[0]
    arrived, grads, act, ggu, packed_back = expert_call(rows_in, weight_in, weight_out)
    back = trade(packed_back)
    packed_y = expert_y_call(act, weight_out)
    d_expert_out = contract(act, grads, 0, 0).astype(BF)[None]
    d_expert_in = contract(arrived, ggu, 0, 0).astype(BF)[None]
    back, packed_y, d_expert_out, d_expert_in = lax.optimization_barrier(
        (back, packed_y, d_expert_out, d_expert_in)
    )
    res, d_residual = combine_grads(routes, back, mixed, gain_row, cotangent, n_exp)

    same_z = [res] + [move(res, over_x(d)) for d in range(1, 4)]
    other_z = move(res, over_z)
    cut = width * 3 // 8
    left_z = [move(v[:, :cut], over_z) for v in same_z[1:]]
    right_z = [move(other_z[:, cut:], over_x(d)) for d in range(1, 4)]
    blocks = [*same_z, other_z, *left_z, *right_z]
    packed_y, *blocks = lax.optimization_barrier((packed_y, *blocks))
    y_back = trade(packed_y)

    w_give, gain_own = plain(
        weight_give_body,
        "weight_give",
        [sds((cols, width), BF), sds((8, width), F32)],
        came,
        ctx_got,
        *blocks,
        flops=16 * tok * cols * width,
    )
    w_grad_got = move(w_give, swap)
    gain_got = move(gain_own, swap)
    out_cols = width // n_ctx
    part = (cols + 32, out_cols)
    sent = plain(
        weight_own_body,
        "weight_own",
        [sds((2,) + part, BF)] * (n_ctx // 2),
        jnp.concatenate([came, lax.axis_index("ctx").reshape(1)]),
        ctx_own,
        w_grad_got,
        gain_own,
        gain_got,
        *blocks,
        flops=16 * tok * cols * width,
        scratch=[pltpu.VMEM((n_ctx,) + part, BF)],
    )
    ctx_mine, ctx_grad_give = plain(
        context_grad_body,
        "context_grad",
        [sds((chips, tok, cols), BF)] * 2,
        came,
        o_weight,
        w_got,
        *blocks,
        flops=32 * tok * cols * width,
    )
    ctx_other = move(ctx_grad_give, swap)
    over_y = [sent[0]]
    for d in range(1, n_ctx // 2):
        around = [(u, (u + 2 * d) % n_ctx) for u in range(n_ctx)]
        over_y.append(lax.ppermute(sent[d], "ctx", around))
    layer_out = combine_out(routes, gate_weights, y_back, mixed, n_exp)
    summed = sum(f.astype(F32) for f in over_y)
    other = summed[1].astype(BF)
    last = lax.ppermute(other, "ctx", [(u, u ^ 1) for u in range(n_ctx)])
    layer_out, last = lax.optimization_barrier((layer_out, last))
    final = summed[0] + last.astype(F32)
    d_o_weight = final[:cols]
    d_gain = jnp.sum(final[cols : cols + 3 * n_ctx].reshape(3, width), axis=0)

    mine = ctx_mine.reshape(chips, 1, tok, cols)
    other = ctx_other.reshape(chips, 1, tok, cols)
    d_context = jnp.where(
        core == 0,
        jnp.concatenate([mine, other], axis=1),
        jnp.concatenate([other, mine], axis=1),
    ).reshape(context.shape)
    return (layer_out, d_context, d_residual, d_o_weight, d_gain, d_expert_in, d_expert_out)


def solution(mesh):
    rows = P(("ctx", "tp"), None)
    experts = P(("ctx", "tp"), None, None)
    in_specs = (P("ctx", "tp"), rows, P("tp", None), P(), rows, rows, experts, experts, rows)
    out_specs = (rows, P("ctx", "tp"), rows, P("tp", "ctx"), P(), experts, experts)
    return jax.shard_map(
        on_device, mesh=mesh, in_specs=in_specs, out_specs=out_specs, check_vma=False
    )
```

profile of v0, /device:TPU:2, one launch (start us, length us, event | category | flops | bytes accessed | tf_op | source)
XLA Modules:
  0.0 334.3 jit_solution(1848271945127834935)
XLA Ops:
  1.3 2.3 collective-permute-done.ctx_got
  3.6 1.5 collective-permute-done.1.w_got
  7.5 2.1 project_first.1
  9.6 4.0 %collective-permute-start.2 = (bf16[512,1024]{1,0:T(8,128)(2,1)S(1)}, bf16[512,1024]{1,0:T(8,128)(2,1)S(1)}, u32[]{:S(2)}, u32[]{:S(2)}) collective-permute-start(bf16[512,1024]{1,0:T(8,128)(2,1)S(1)} %get-tuple-element.56), channel_id=1, source_target_pairs={{0,2},{1,3},{2,0},{3,1},{4,6},{5,7},{6,4},{7,5},{8,10},{9,11},{10,... | collective-permute-start | bytes 3145736 | tf_op jit(solution)/shard_map/ppermute | solution.py:614
  13.6 1.5 collective-permute-start.3
  16.2 2.2 collective-permute-start.5
  18.3 1.5 project_keep.1
  19.9 8.5 %collective-permute-done.3.got_1 = bf16[256,1024]{1,0:T(8,128)(2,1)S(1)} collective-permute-done((bf16[256,1024]{1,0:T(8,128)(2,1)S(1)}, bf16[256,1024]{1,0:T(8,128)(2,1)S(1)}, u32[]{:S(2)}, u32[]{:S(2)}) %collective-permute-start.3) | collective-permute-done | bytes 524320 | tf_op jit(solution)/shard_map/ppermute | solution.py:614
  28.4 3.0 collective-permute-done.4.got_2
  31.4 9.1 %collective-permute-done.5.got_3 = bf16[256,1024]{1,0:T(8,128)(2,1)S(1)} collective-permute-done((bf16[256,1024]{1,0:T(8,128)(2,1)S(1)}, bf16[256,1024]{1,0:T(8,128)(2,1)S(1)}, u32[]{:S(2)}, u32[]{:S(2)}) %collective-permute-start.5) | collective-permute-done | bytes 524320 | tf_op jit(solution)/shard_map/ppermute | solution.py:614
  40.5 1.6 add.203
  42.2 1.3 collective-permute-start.6
  43.5 1.5 collective-permute-start.7
  44.9 1.7 collective-permute-start.8
  47.2 2.6 pack_grads.1.refs_6_
  49.8 1.8 collective-permute-done.6.refs_0_
  51.6 2.8 collective-permute-done.7.refs_1_
  54.4 3.0 collective-permute-done.8.refs_2_
  57.4 3.3 norm_pack.1
  60.7 81.9 %all_to_all.15 = bf16[128,8,3072]{2,1,0:T(8,128)(2,1)} all-to-all(bf16[128,8,3072]{2,1,0:T(8,128)(2,1)S(1)} %bitcast.42), channel_id=1, replica_groups=mesh['ctx'=8,'tp'=16] {'ctx','tp'}, dimensions={0} | all-to-all | bytes 12582912 | tf_op jit(solution)/shard_map/all_to_all | solution.py:585
  142.6 24.7 %expert.1 = (bf16[768,2048]{1,0:T(8,128)(2,1)}, bf16[768,2048]{1,0:T(8,128)(2,1)}, bf16[768,768]{1,0:T(8,128)(2,1)}, bf16[768,1536]{1,0:T(8,128)(2,1)}, bf16[1024,1536]{1,0:T(8,128)(2,1)}) custom-call(bf16[1024,3072]{1,0:T(8,128)(2,1)} %bitcast.48, bf16[1024,3072]{1,0:T(8,128)(2,1)} %bitcast.49, bf16[2048,1536]{1,0:T(8,128)(2,1)} %bitcast.54, ...), custom_call_target="tpu_custom_call" | custom-call | flops 12079595520 | bytes 22020096 | tf_op jit(solution)/shard_map/expert/pallas_call | solution.py:395
  167.3 6.5 %all-to-all-start.1 = ((bf16[128,8,1536]{2,1,0:T(8,128)(2,1)}), bf16[128,8,1536]{2,1,0:T(8,128)(2,1)S(1)}, u32[]{:S(2)}, u32[]{:S(2)}) async-start(bf16[128,8,1536]{2,1,0:T(8,128)(2,1)} %bitcast.51), calls=%async_computation.1 | async-start | bytes 6291456 | tf_op jit(solution)/shard_map/all_to_all | solution.py:585
  173.9 7.9 %expert_y.1 = bf16[1024,1536]{1,0:T(8,128)(2,1)} custom-call(bf16[768,768]{1,0:T(8,128)(2,1)} %get-tuple-element.68.act, bf16[768,2048]{1,0:T(8,128)(2,1)} %bitcast.56), custom_call_target="tpu_custom_call" | custom-call | flops 2415919104 | bytes 9437184 | tf_op jit(solution)/shard_map/expert_y/pallas_call | solution.py:435
  181.8 4.0 %fusion.1 = bf16[1,768,2048]{2,1,0:T(8,128)(2,1)} fusion(bf16[768,768]{1,0:T(8,128)(2,1)S(1)} %copy-done.24, bf16[768,2048]{1,0:T(8,128)(2,1)S(1)} %copy-done.25), kind=kOutput, calls=%fused_computation.3 | convolution fusion | flops 2417491968 | bytes 7471104 | tf_op jit(solution)/shard_map/dot_general | solution.py:20
  185.8 7.1 %fusion = bf16[1,2048,1536]{2,1,0:T(8,128)(2,1)} fusion(bf16[768,2048]{1,0:T(8,128)(2,1)S(1)} %copy-done.26, bf16[768,1536]{1,0:T(8,128)(2,1)S(1)} %copy-done.27), kind=kOutput, calls=%fused_computation.1 | convolution fusion | flops 4834983936 | bytes 11796480 | tf_op jit(solution)/shard_map/dot_general | solution.py:20
  192.9 21.8 %all-to-all-done.1 = bf16[128,8,1536]{2,1,0:T(8,128)(2,1)S(1)} async-done(((bf16[128,8,1536]{2,1,0:T(8,128)(2,1)}), bf16[128,8,1536]{2,1,0:T(8,128)(2,1)S(1)}, u32[]{:S(2)}, u32[]{:S(2)}) %all-to-all-start.1) | async-done | bytes 3145760 | tf_op jit(solution)/shard_map/all_to_all | solution.py:585
  216.7 2.6 combine_grads.1
  219.3 1.2 collective-permute-start.10
  220.8 3.5 %collective-permute-start.11 = (bf16[144,2048]{1,0:T(8,128)(2,1)S(1)}, bf16[144,2048]{1,0:T(8,128)(2,1)S(1)}, u32[]{:S(2)}, u32[]{:S(2)}) collective-permute-start(bf16[144,2048]{1,0:T(8,128)(2,1)S(1)} %get-tuple-element.77.refs_0_), channel_id=1, source_target_pairs={{0,8},{1,9},{2,10},{3,11},{4,12},{5,13},{6,14},{7,15},{8,0},{9,1},... | collective-permute-start | bytes 1769480 | tf_op jit(solution)/shard_map/ppermute | solution.py:614
  224.4 11.2 %collective-permute-done.10.refs_1_ = bf16[144,2048]{1,0:T(8,128)(2,1)S(1)} collective-permute-done((bf16[144,2048]{1,0:T(8,128)(2,1)S(1)}, bf16[144,2048]{1,0:T(8,128)(2,1)S(1)}, u32[]{:S(2)}, u32[]{:S(2)}) %collective-permute-start.10) | collective-permute-done | bytes 589856 | tf_op jit(solution)/shard_map/ppermute | solution.py:614
  237.6 15.8 %collective-permute-start.18 = (bf16[144,1280]{1,0:T(8,128)(2,1)S(1)}, bf16[144,1280]{1,0:T(8,128)(2,1)}, u32[]{:S(2)}, u32[]{:S(2)}) collective-permute-start(bf16[144,1280]{1,0:T(8,128)(2,1)S(1)} %slice.38), channel_id=1, source_target_pairs={{0,8},{1,9},{2,10},{3,11},{4,12},{5,13},{6,14},{7,15},{8,0},{9,1},... | collective-permute-start | bytes 1105928 | tf_op jit(solution)/shard_map/ppermute | solution.py:614
  253.4 1.3 collective-permute-start.15
  254.8 2.4 collective-permute-start.16
  257.2 5.0 %collective-permute-done.15.refs_6_ = bf16[144,768]{1,0:T(8,128)(2,1)} collective-permute-done((bf16[144,768]{1,0:T(8,128)(2,1)S(1)}, bf16[144,768]{1,0:T(8,128)(2,1)}, u32[]{:S(2)}, u32[]{:S(2)}) %collective-permute-start.15) | collective-permute-done | bytes 221216 | tf_op jit(solution)/shard_map/ppermute | solution.py:614
  262.1 2.4 collective-permute-done.16.refs_7_
  264.5 2.2 collective-permute-done.19.refs_10_
  266.7 6.4 %all-to-all-start.2 = ((bf16[128,8,1536]{2,1,0:T(8,128)(2,1)}), bf16[128,8,1536]{2,1,0:T(8,128)(2,1)S(1)}, u32[]{:S(2)}, u32[]{:S(2)}) async-start(bf16[128,8,1536]{2,1,0:T(8,128)(2,1)} %bitcast.50), calls=%async_computation.2 | async-start | bytes 6291456 | tf_op jit(solution)/shard_map/all_to_all | solution.py:585
  273.9 4.9 %weight_give.1 = (bf16[256,2048]{1,0:T(8,128)(2,1)}, f32[8,2048]{1,0:T(8,128)}) custom-call(s32[8]{0:T(128)} %stack.65.order, bf16[16,128,256]{2,1,0:T(8,128)(2,1)} %copy-done.1, bf16[144,2048]{1,0:T(8,128)(2,1)} %copy-done.2, bf16[144,2048]{1,0:T(8,128)(2,1)} %copy-done.12, bf16[144,2048]{1,0:T(8,128)(2,1)} %copy-done.13, bf16[144,2048]{1,0:T(8,128)(2,1)} %copy-done.14, ...), custom_call_target="tpu_custom_call" | custom-call | flops 1073741824 | bytes 6881280 | tf_op jit(solution)/shard_map/weight_give/pallas_call | solution.py:492
  279.3 6.3 %context_grad.1 = (bf16[8,128,256]{2,1,0:T(8,128)(2,1)}, bf16[8,128,256]{2,1,0:T(8,128)(2,1)}) custom-call(s32[8]{0:T(128)} %stack.65.order, bf16[256,2048]{1,0:T(8,128)(2,1)} %w_own.5, bf16[256,2048]{1,0:T(8,128)(2,1)} %copy-done.4, bf16[144,2048]{1,0:T(8,128)(2,1)} %copy-done.2, bf16[144,2048]{1,0:T(8,128)(2,1)} %copy-done.12, ...), custom_call_target="tpu_custom_call" | custom-call | flops 2147483648 | bytes 7864320 | tf_op jit(solution)/shard_map/context_grad/pallas_call | solution.py:492
  288.2 5.3 %weight_own.1 = (bf16[2,288,256]{2,1,0:T(8,128)(2,1)}, bf16[2,288,256]{2,1,0:T(8,128)(2,1)}, bf16[2,288,256]{2,1,0:T(8,128)(2,1)}, bf16[2,288,256]{2,1,0:T(8,128)(2,1)}) custom-call(s32[9]{0:T(128)} %concatenate.10.order, bf16[16,128,256]{2,1,0:T(8,128)(2,1)} %bitcast.44, bf16[256,2048]{1,0:T(8,128)(2,1)} %collective-permute-done.20.got, ...), custom_call_target="tpu_custom_call" | custom-call | flops 1073741824 | bytes 8126464 | tf_op jit(solution)/shard_map/weight_own/pallas_call | solution.py:492
  293.5 1.5 collective-permute-start.22
  295.0 2.7 collective-permute-start.23
  297.8 1.4 collective-permute-start.24
  299.2 1.8 maximum_select_fusion
  302.0 21.5 %collective-permute-done.22 = bf16[2,288,256]{2,1,0:T(8,128)(2,1)} collective-permute-done((bf16[2,288,256]{2,1,0:T(8,128)(2,1)}, bf16[2,288,256]{2,1,0:T(8,128)(2,1)}, u32[]{:S(2)}, u32[]{:S(2)}) %collective-permute-start.22) | collective-permute-done | bytes 294944 | tf_op jit(solution)/shard_map/ppermute | solution.py:719
  323.5 1.3 convert_add_fusion
  325.6 2.1 collective-permute-start.25
  328.7 3.3 combine_out.1
  (100 shorter events, 18.4 us)
Async XLA Ops:
  0.6 3.0 collective-permute-start
  0.7 4.4 %collective-permute-start.1 = (bf16[256,2048]{1,0:T(8,128)(2,1)}, bf16[256,2048]{1,0:T(8,128)(2,1)S(1)}, u32[]{:S(2)}, u32[]{:S(2)}) collective-permute-start(bf16[256,2048]{1,0:T(8,128)(2,1)} %w_own.5), channel_id=1, source_target_pairs={{0,1},{1,0},{2,3},{3,2},{4,5},{5,4},{6,7},{7,6},{8,9},{9,8},{10,11... | collective-permute-start | bytes 3145736 | tf_op jit(solution)/shard_map/ppermute | solution.py:614
  3.6 16.3 %copy-start.1 = (bf16[16,128,256]{2,1,0:T(8,128)(2,1)}, bf16[16,128,256]{2,1,0:T(8,128)(2,1)S(1)}, u32[]{:S(2)}) copy-start(bf16[16,128,256]{2,1,0:T(8,128)(2,1)S(1)} %collective-permute-done.ctx_got) | copy-start | bytes 3145732
  7.5 12.3 %copy-start.4 = (bf16[256,2048]{1,0:T(8,128)(2,1)}, bf16[256,2048]{1,0:T(8,128)(2,1)S(1)}, u32[]{:S(2)}) copy-start(bf16[256,2048]{1,0:T(8,128)(2,1)S(1)} %collective-permute-done.1.w_got) | copy-start | bytes 3145732
  9.6 30.9 %collective-permute-start.2 = (bf16[512,1024]{1,0:T(8,128)(2,1)S(1)}, bf16[512,1024]{1,0:T(8,128)(2,1)S(1)}, u32[]{:S(2)}, u32[]{:S(2)}) collective-permute-start(bf16[512,1024]{1,0:T(8,128)(2,1)S(1)} %get-tuple-element.56), channel_id=1, source_target_pairs={{0,2},{1,3},{2,0},{3,1},{4,6},{5,7},{6,4},{7,5},{8,10},{9,11},{10,... | collective-permute-start | bytes 3145736 | tf_op jit(solution)/shard_map/ppermute | solution.py:614
  13.6 14.8 %collective-permute-start.3 = (bf16[256,1024]{1,0:T(8,128)(2,1)S(1)}, bf16[256,1024]{1,0:T(8,128)(2,1)S(1)}, u32[]{:S(2)}, u32[]{:S(2)}) collective-permute-start(bf16[256,1024]{1,0:T(8,128)(2,1)S(1)} %get-tuple-element.57), channel_id=1, source_target_pairs={{0,4},{1,5},{2,6},{3,7},{4,8},{5,9},{6,10},{7,11},{8,12},{9,13},{1... | collective-permute-start | bytes 1572872 | tf_op jit(solution)/shard_map/ppermute | solution.py:614
  15.1 16.4 %collective-permute-start.4 = (bf16[256,1024]{1,0:T(8,128)(2,1)S(1)}, bf16[256,1024]{1,0:T(8,128)(2,1)S(1)}, u32[]{:S(2)}, u32[]{:S(2)}) collective-permute-start(bf16[256,1024]{1,0:T(8,128)(2,1)S(1)} %get-tuple-element.58), channel_id=1, source_target_pairs={{0,8},{1,9},{2,10},{3,11},{4,12},{5,13},{6,14},{7,15},{8,0},{9,1},... | collective-permute-start | bytes 1572872 | tf_op jit(solution)/shard_map/ppermute | solution.py:614
  16.2 24.4 %collective-permute-start.5 = (bf16[256,1024]{1,0:T(8,128)(2,1)S(1)}, bf16[256,1024]{1,0:T(8,128)(2,1)S(1)}, u32[]{:S(2)}, u32[]{:S(2)}) collective-permute-start(bf16[256,1024]{1,0:T(8,128)(2,1)S(1)} %get-tuple-element.59), channel_id=1, source_target_pairs={{0,12},{1,13},{2,14},{3,15},{4,0},{5,1},{6,2},{7,3},{8,4},{9,5},{1... | collective-permute-start | bytes 1572872 | tf_op jit(solution)/shard_map/ppermute | solution.py:614
  19.9 27.1 %copy-start.22 = (s32[128,4]{0,1:T(4,128)S(1)}, s32[128,4]{0,1:T(4,128)}, u32[]{:S(2)}) copy-start(s32[128,4]{0,1:T(4,128)} %param.13) | copy-start | bytes 6148
  19.9 27.2 %copy-start.23 = (f32[128,4]{0,1:T(4,128)S(1)}, f32[128,4]{0,1:T(4,128)}, u32[]{:S(2)}) copy-start(f32[128,4]{0,1:T(4,128)} %param.14) | copy-start | bytes 6148
  19.9 27.3 %copy-start.21 = (bf16[2048]{0:T(1024)(128)(2,1)S(1)}, bf16[2048]{0:T(1024)(128)(2,1)}, u32[]{:S(2)}) copy-start(bf16[2048]{0:T(1024)(128)(2,1)} %param.12) | copy-start | bytes 12292
  19.9 27.3 %copy-start.6 = (bf16[128,2048]{1,0:T(8,128)(2,1)S(1)}, bf16[128,2048]{1,0:T(8,128)(2,1)}, u32[]{:S(2)}) copy-start(bf16[128,2048]{1,0:T(8,128)(2,1)} %cot.3) | copy-start | bytes 1572868
  42.2 15.3 %copy-start.5 = (bf16[128,2048]{1,0:T(8,128)(2,1)S(1)}, bf16[128,2048]{1,0:T(8,128)(2,1)}, u32[]{:S(2)}) copy-start(bf16[128,2048]{1,0:T(8,128)(2,1)} %refs_4_.1) | copy-start | bytes 1572868
  42.2 9.5 %collective-permute-start.6 = (bf16[128,1024]{1,0:T(8,128)(2,1)}, bf16[128,1024]{1,0:T(8,128)(2,1)S(1)}, u32[]{:S(2)}, u32[]{:S(2)}) collective-permute-start(bf16[128,1024]{1,0:T(8,128)(2,1)} %get-tuple-element.62), channel_id=1, source_target_pairs={{0,4},{1,5},{2,6},{3,7},{4,8},{5,9},{6,10},{7,11},{8,12},{9,13},{1... | collective-permute-start | bytes 786440 | tf_op jit(solution)/shard_map/ppermute | solution.py:614
  43.5 11.0 %collective-permute-start.7 = (bf16[128,1024]{1,0:T(8,128)(2,1)}, bf16[128,1024]{1,0:T(8,128)(2,1)S(1)}, u32[]{:S(2)}, u32[]{:S(2)}) collective-permute-start(bf16[128,1024]{1,0:T(8,128)(2,1)} %get-tuple-element.63), channel_id=1, source_target_pairs={{0,8},{1,9},{2,10},{3,11},{4,12},{5,13},{6,14},{7,15},{8,0},{9,1},... | collective-permute-start | bytes 786440 | tf_op jit(solution)/shard_map/ppermute | solution.py:614
  44.9 12.5 %collective-permute-start.8 = (bf16[128,1024]{1,0:T(8,128)(2,1)}, bf16[128,1024]{1,0:T(8,128)(2,1)S(1)}, u32[]{:S(2)}, u32[]{:S(2)}) collective-permute-start(bf16[128,1024]{1,0:T(8,128)(2,1)} %get-tuple-element.64), channel_id=1, source_target_pairs={{0,12},{1,13},{2,14},{3,15},{4,0},{5,1},{6,2},{7,3},{8,4},{9,5},{1... | collective-permute-start | bytes 786440 | tf_op jit(solution)/shard_map/ppermute | solution.py:614
  46.6 10.8 %collective-permute-start.9 = (bf16[128,1024]{1,0:T(8,128)(2,1)S(1)}, bf16[128,1024]{1,0:T(8,128)(2,1)S(1)}, u32[]{:S(2)}, u32[]{:S(2)}) collective-permute-start(bf16[128,1024]{1,0:T(8,128)(2,1)S(1)} %get-tuple-element.65), channel_id=1, source_target_pairs={{0,2},{1,3},{2,0},{3,1},{4,6},{5,7},{6,4},{7,5},{8,10},{9,11},{10,... | collective-permute-start | bytes 786440 | tf_op jit(solution)/shard_map/ppermute | solution.py:614
  60.7 81.9 %copy-start.8 = (bf16[128,2048]{1,0:T(8,128)(2,1)}, bf16[128,2048]{1,0:T(8,128)(2,1)S(1)}, u32[]{:S(2)}) copy-start(bf16[128,2048]{1,0:T(8,128)(2,1)S(1)} %get-tuple-element.74.mixed_ref.mixed) | copy-start | bytes 1572868
  167.3 47.3 %all-to-all-start.1 = ((bf16[128,8,1536]{2,1,0:T(8,128)(2,1)}), bf16[128,8,1536]{2,1,0:T(8,128)(2,1)S(1)}, u32[]{:S(2)}, u32[]{:S(2)}) async-start(bf16[128,8,1536]{2,1,0:T(8,128)(2,1)} %bitcast.51), calls=%async_computation.1 | async-start | bytes 6291456 | tf_op jit(solution)/shard_map/all_to_all | solution.py:585
  173.9 7.9 %copy-start.24 = (bf16[768,768]{1,0:T(8,128)(2,1)S(1)}, bf16[768,768]{1,0:T(8,128)(2,1)}, u32[]{:S(2)}) copy-start(bf16[768,768]{1,0:T(8,128)(2,1)} %get-tuple-element.68.act) | copy-start | bytes 3538948
  173.9 7.9 %copy-start.25 = (bf16[768,2048]{1,0:T(8,128)(2,1)S(1)}, bf16[768,2048]{1,0:T(8,128)(2,1)}, u32[]{:S(2)}) copy-start(bf16[768,2048]{1,0:T(8,128)(2,1)} %get-tuple-element.69) | copy-start | bytes 9437188
  181.8 4.0 %copy-start.26 = (bf16[768,2048]{1,0:T(8,128)(2,1)S(1)}, bf16[768,2048]{1,0:T(8,128)(2,1)}, u32[]{:S(2)}) copy-start(bf16[768,2048]{1,0:T(8,128)(2,1)} %get-tuple-element.70) | copy-start | bytes 9437188
  181.8 4.0 %copy-start.27 = (bf16[768,1536]{1,0:T(8,128)(2,1)S(1)}, bf16[768,1536]{1,0:T(8,128)(2,1)}, u32[]{:S(2)}) copy-start(bf16[768,1536]{1,0:T(8,128)(2,1)} %get-tuple-element.71) | copy-start | bytes 7077892
  219.3 5.0 %copy-start.2 = (bf16[144,2048]{1,0:T(8,128)(2,1)}, bf16[144,2048]{1,0:T(8,128)(2,1)S(1)}, u32[]{:S(2)}) copy-start(bf16[144,2048]{1,0:T(8,128)(2,1)S(1)} %get-tuple-element.77.refs_0_) | copy-start | bytes 1769476
  219.3 16.3 %collective-permute-start.10 = (bf16[144,2048]{1,0:T(8,128)(2,1)S(1)}, bf16[144,2048]{1,0:T(8,128)(2,1)S(1)}, u32[]{:S(2)}, u32[]{:S(2)}) collective-permute-start(bf16[144,2048]{1,0:T(8,128)(2,1)S(1)} %get-tuple-element.77.refs_0_), channel_id=1, source_target_pairs={{0,4},{1,5},{2,6},{3,7},{4,8},{5,9},{6,10},{7,11},{8,12},{9,13},{1... | collective-permute-start | bytes 1769480 | tf_op jit(solution)/shard_map/ppermute | solution.py:614
  220.6 16.8 %collective-permute-start.13 = (bf16[144,2048]{1,0:T(8,128)(2,1)S(1)}, bf16[144,2048]{1,0:T(8,128)(2,1)S(1)}, u32[]{:S(2)}, u32[]{:S(2)}) collective-permute-start(bf16[144,2048]{1,0:T(8,128)(2,1)S(1)} %get-tuple-element.77.refs_0_), channel_id=1, source_target_pairs={{0,2},{1,3},{2,0},{3,1},{4,6},{5,7},{6,4},{7,5},{8,10},{9,11},{10,... | collective-permute-start | bytes 1769480 | tf_op jit(solution)/shard_map/ppermute | solution.py:614
  220.8 32.6 %collective-permute-start.11 = (bf16[144,2048]{1,0:T(8,128)(2,1)S(1)}, bf16[144,2048]{1,0:T(8,128)(2,1)S(1)}, u32[]{:S(2)}, u32[]{:S(2)}) collective-permute-start(bf16[144,2048]{1,0:T(8,128)(2,1)S(1)} %get-tuple-element.77.refs_0_), channel_id=1, source_target_pairs={{0,8},{1,9},{2,10},{3,11},{4,12},{5,13},{6,14},{7,15},{8,0},{9,1},... | collective-permute-start | bytes 1769480 | tf_op jit(solution)/shard_map/ppermute | solution.py:614
  224.3 29.1 %collective-permute-start.12 = (bf16[144,2048]{1,0:T(8,128)(2,1)S(1)}, bf16[144,2048]{1,0:T(8,128)(2,1)S(1)}, u32[]{:S(2)}, u32[]{:S(2)}) collective-permute-start(bf16[144,2048]{1,0:T(8,128)(2,1)S(1)} %get-tuple-element.77.refs_0_), channel_id=1, source_target_pairs={{0,12},{1,13},{2,14},{3,15},{4,0},{5,1},{6,2},{7,3},{8,4},{9,5},{1... | collective-permute-start | bytes 1769480 | tf_op jit(solution)/shard_map/ppermute | solution.py:614
  236.4 18.3 %collective-permute-start.14 = (bf16[144,768]{1,0:T(8,128)(2,1)S(1)}, bf16[144,768]{1,0:T(8,128)(2,1)S(1)}, u32[]{:S(2)}, u32[]{:S(2)}) collective-permute-start(bf16[144,768]{1,0:T(8,128)(2,1)S(1)} %slice.35), channel_id=1, source_target_pairs={{0,2},{1,3},{2,0},{3,1},{4,6},{5,7},{6,4},{7,5},{8,10},{9,11},{10,... | collective-permute-start | bytes 663560 | tf_op jit(solution)/shard_map/ppermute | solution.py:614
  237.4 16.0 %copy-start.11 = (bf16[144,2048]{1,0:T(8,128)(2,1)}, bf16[144,2048]{1,0:T(8,128)(2,1)S(1)}, u32[]{:S(2)}) copy-start(bf16[144,2048]{1,0:T(8,128)(2,1)S(1)} %collective-permute-done.13.refs_4_) | copy-start | bytes 1769476
  237.4 27.1 %collective-permute-start.17 = (bf16[144,1280]{1,0:T(8,128)(2,1)S(1)}, bf16[144,1280]{1,0:T(8,128)(2,1)}, u32[]{:S(2)}, u32[]{:S(2)}) collective-permute-start(bf16[144,1280]{1,0:T(8,128)(2,1)S(1)} %slice.38), channel_id=1, source_target_pairs={{0,4},{1,5},{2,6},{3,7},{4,8},{5,9},{6,10},{7,11},{8,12},{9,13},{1... | collective-permute-start | bytes 1105928 | tf_op jit(solution)/shard_map/ppermute | solution.py:614
  237.6 26.9 %collective-permute-start.18 = (bf16[144,1280]{1,0:T(8,128)(2,1)S(1)}, bf16[144,1280]{1,0:T(8,128)(2,1)}, u32[]{:S(2)}, u32[]{:S(2)}) collective-permute-start(bf16[144,1280]{1,0:T(8,128)(2,1)S(1)} %slice.38), channel_id=1, source_target_pairs={{0,8},{1,9},{2,10},{3,11},{4,12},{5,13},{6,14},{7,15},{8,0},{9,1},... | collective-permute-start | bytes 1105928 | tf_op jit(solution)/shard_map/ppermute | solution.py:614
  253.3 1.4 copy-start.13
  253.3 13.4 %collective-permute-start.19 = (bf16[144,1280]{1,0:T(8,128)(2,1)S(1)}, bf16[144,1280]{1,0:T(8,128)(2,1)}, u32[]{:S(2)}, u32[]{:S(2)}) collective-permute-start(bf16[144,1280]{1,0:T(8,128)(2,1)S(1)} %slice.38), channel_id=1, source_target_pairs={{0,12},{1,13},{2,14},{3,15},{4,0},{5,1},{6,2},{7,3},{8,4},{9,5},{1... | collective-permute-start | bytes 1105928 | tf_op jit(solution)/shard_map/ppermute | solution.py:614
  253.4 8.7 %collective-permute-start.15 = (bf16[144,768]{1,0:T(8,128)(2,1)S(1)}, bf16[144,768]{1,0:T(8,128)(2,1)}, u32[]{:S(2)}, u32[]{:S(2)}) collective-permute-start(bf16[144,768]{1,0:T(8,128)(2,1)S(1)} %slice.36), channel_id=1, source_target_pairs={{0,2},{1,3},{2,0},{3,1},{4,6},{5,7},{6,4},{7,5},{8,10},{9,11},{10,... | collective-permute-start | bytes 663560 | tf_op jit(solution)/shard_map/ppermute | solution.py:614
  254.8 11.9 %copy-start.17 = (bf16[144,768]{1,0:T(8,128)(2,1)}, bf16[144,768]{1,0:T(8,128)(2,1)S(1)}, u32[]{:S(2)}) copy-start(bf16[144,768]{1,0:T(8,128)(2,1)S(1)} %collective-permute-done.14.refs_5_) | copy-start | bytes 663556
  254.8 9.7 %collective-permute-start.16 = (bf16[144,768]{1,0:T(8,128)(2,1)S(1)}, bf16[144,768]{1,0:T(8,128)(2,1)}, u32[]{:S(2)}, u32[]{:S(2)}) collective-permute-start(bf16[144,768]{1,0:T(8,128)(2,1)S(1)} %slice.37), channel_id=1, source_target_pairs={{0,2},{1,3},{2,0},{3,1},{4,6},{5,7},{6,4},{7,5},{8,10},{9,11},{10,... | collective-permute-start | bytes 663560 | tf_op jit(solution)/shard_map/ppermute | solution.py:614
  266.7 61.0 %all-to-all-start.2 = ((bf16[128,8,1536]{2,1,0:T(8,128)(2,1)}), bf16[128,8,1536]{2,1,0:T(8,128)(2,1)S(1)}, u32[]{:S(2)}, u32[]{:S(2)}) async-start(bf16[128,8,1536]{2,1,0:T(8,128)(2,1)} %bitcast.50), calls=%async_computation.2 | async-start | bytes 6291456 | tf_op jit(solution)/shard_map/all_to_all | solution.py:585
  278.8 7.2 %copy-start.19 = (f32[8,2048]{1,0:T(8,128)S(1)}, f32[8,2048]{1,0:T(8,128)}, u32[]{:S(2)}) copy-start(f32[8,2048]{1,0:T(8,128)} %get-tuple-element.89.gain_own) | copy-start | bytes 196612
  278.8 8.8 %collective-permute-start.20 = (bf16[256,2048]{1,0:T(8,128)(2,1)}, bf16[256,2048]{1,0:T(8,128)(2,1)}, u32[]{:S(2)}, u32[]{:S(2)}) collective-permute-start(bf16[256,2048]{1,0:T(8,128)(2,1)} %get-tuple-element.88), channel_id=1, source_target_pairs={{0,1},{1,0},{2,3},{3,2},{4,5},{5,4},{6,7},{7,6},{8,9},{9,8},{10,11... | collective-permute-start | bytes 3145736 | tf_op jit(solution)/shard_map/ppermute | solution.py:614
  285.6 13.6 %collective-permute-start.26 = (bf16[8,128,256]{2,1,0:T(8,128)(2,1)}, bf16[8,128,256]{2,1,0:T(8,128)(2,1)}, u32[]{:S(2)}, u32[]{:S(2)}) collective-permute-start(bf16[8,128,256]{2,1,0:T(8,128)(2,1)} %get-tuple-element.96), channel_id=1, source_target_pairs={{0,1},{1,0},{2,3},{3,2},{4,5},{5,4},{6,7},{7,6},{8,9},{9,8},{10,11... | collective-permute-start | bytes 1572872 | tf_op jit(solution)/shard_map/ppermute | solution.py:614
  286.0 1.6 collective-permute-start.21
  293.5 29.9 %collective-permute-start.22 = (bf16[2,288,256]{2,1,0:T(8,128)(2,1)}, bf16[2,288,256]{2,1,0:T(8,128)(2,1)}, u32[]{:S(2)}, u32[]{:S(2)}) collective-permute-start(bf16[2,288,256]{2,1,0:T(8,128)(2,1)} %get-tuple-element.91), channel_id=1, source_target_pairs={{0,32},{16,48},{32,64},{48,80},{64,96},{80,112},{96,0},{112,16},{1... | collective-permute-start | bytes 884744 | tf_op jit(solution)/shard_map/ppermute | solution.py:719
  295.0 28.5 %collective-permute-start.23 = (bf16[2,288,256]{2,1,0:T(8,128)(2,1)}, bf16[2,288,256]{2,1,0:T(8,128)(2,1)}, u32[]{:S(2)}, u32[]{:S(2)}) collective-permute-start(bf16[2,288,256]{2,1,0:T(8,128)(2,1)} %get-tuple-element.92), channel_id=1, source_target_pairs={{0,64},{16,80},{32,96},{48,112},{64,0},{80,16},{96,32},{112,48},{1... | collective-permute-start | bytes 884744 | tf_op jit(solution)/shard_map/ppermute | solution.py:719
  297.8 25.7 %collective-permute-start.24 = (bf16[2,288,256]{2,1,0:T(8,128)(2,1)}, bf16[2,288,256]{2,1,0:T(8,128)(2,1)}, u32[]{:S(2)}, u32[]{:S(2)}) collective-permute-start(bf16[2,288,256]{2,1,0:T(8,128)(2,1)} %get-tuple-element.93), channel_id=1, source_target_pairs={{0,96},{16,112},{32,0},{48,16},{64,32},{80,48},{96,64},{112,80},{1... | collective-permute-start | bytes 884744 | tf_op jit(solution)/shard_map/ppermute | solution.py:719
  299.2 24.3 %copy-start.18 = (bf16[2,288,256]{2,1,0:T(8,128)(2,1)S(1)}, bf16[2,288,256]{2,1,0:T(8,128)(2,1)}, u32[]{:S(2)}) copy-start(bf16[2,288,256]{2,1,0:T(8,128)(2,1)} %get-tuple-element.90) | copy-start | bytes 884740
  325.6 6.4 %collective-permute-start.25 = (bf16[288,256]{1,0:T(8,128)(2,1)S(1)}, bf16[288,256]{1,0:T(8,128)(2,1)}, u32[]{:S(2)}, u32[]{:S(2)}) collective-permute-start(bf16[288,256]{1,0:T(8,128)(2,1)S(1)} %fusion.3), channel_id=1, source_target_pairs={{0,16},{16,0},{32,48},{48,32},{64,80},{80,64},{96,112},{112,96},{1... | collective-permute-start | bytes 442376 | tf_op jit(solution)/shard_map/ppermute | solution.py:723
  328.7 3.3 copy-start.16
  (9 other events, 9.2 us)
where the time goes:
time: 335 us; the launch traced here: 334 us
  waiting for transfers between devices  96.8 us (29%)
  blocking collectives  81.9 us (24%)
  Pallas kernels  66.1 us (20%)
  starting transfers between devices  61.3 us (18%)
  local copies, waits for them, and re-layouts  11.4 us (3%)
  matrix products  11.1 us (3%)
  other arithmetic  4.66 us (1%)
    all_to_all x1, blocking collectives, trade(): lax.all_to_all(shaped, ('ctx', 'tp'), split_axis=0, concat_axis=0, tiled=...  81.9 us
    ppermute x23, waiting for transfers between devices, move(): return lax.ppermute(values, 'tp', perm)  53.6 us
    ppermute x23, starting transfers between devices, move(): return lax.ppermute(values, 'tp', perm)  40.7 us
    pallas_call x1, Pallas kernels, expert_call(): call(expert_body, 'expert', (sds((real * steps, width), BF), sds((real *...  24.7 us
    pallas_call x6, Pallas kernels, plain(): call(body, name, tuple(outs), (1,), [pl.BlockSpec(memory_space=pltpu.SMEM...  21.8 us
    all_to_all x2, waiting for transfers between devices, trade(): lax.all_to_all(shaped, ('ctx', 'tp'), split_axis=0, concat_axis=0, tiled=...  21.8 us
    ppermute x3, waiting for transfers between devices, on_device(): over_y.append(lax.ppermute(sent[d], 'ctx', around))  21.5 us
    all_to_all x2, starting transfers between devices, trade(): lax.all_to_all(shaped, ('ctx', 'tp'), split_axis=0, concat_axis=0, tiled=...  12.9 us
  transfers between devices with their start and end apart: 29, of which 15 were waited for; matrix products, arithmetic and copies ran while one was open for 5% of the time, Pallas kernels for 10%

commit v1 on v0

--- a/solution.py
+++ b/solution.py
@@ -13,6 +13,7 @@
 GROUP = 8
 PACK = 3
 MIB = 1024 * 1024
+LANES = 128
 BIG = ("expert", "expert_y", "weight_give", "weight_own", "context_grad")
 
 
@@ -262,19 +263,20 @@
     inv_rms = lax.rsqrt(jnp.mean(mixed * mixed, axis=-1, keepdims=True) + 1e-06)
     normed = mixed * inv_rms
     d_gain = jnp.sum(grad_h * normed, axis=0, keepdims=True)
-    high, middle, low = thirds(d_gain)
-    row = iota((16, width), 0)
-    gain_rows = jnp.where(row == 0, high.astype(F32), 0.0)
-    gain_rows = jnp.where(row == 1, middle.astype(F32), gain_rows)
-    gain_rows = jnp.where(row == 2, low.astype(F32), gain_rows)
+    gain_cols = jnp.zeros((tok, LANES), F32)
+    row = iota((tok, LANES), 0)
+    per = width // LANES
+    for p, part in enumerate(thirds(d_gain)):
+        for q in range(per):
+            piece = part[:, q * LANES : (q + 1) * LANES].astype(F32)
+            gain_cols = jnp.where(row == p * per + q, piece, gain_cols)
     grad_n = grad_h * gain[...].astype(F32)
     inner = jnp.mean(grad_n * normed, axis=-1, keepdims=True)
     d_res = cot[...].astype(F32) + inv_rms * (grad_n - normed * inner)
     d_res = d_res.astype(BF)
-    gain_rows = gain_rows.astype(BF)
     res_out[...] = d_res
-    out[0:tok, :] = d_res
-    out[tok : tok + 16, :] = gain_rows
+    out[:, :width] = d_res
+    out[:, width:] = gain_cols.astype(BF)
 
 
 def combine_grads(routes, packed, mixed, gain, cot, n_exp):
@@ -282,10 +284,10 @@
     return call(
         functools.partial(combine_grads_body, n_exp),
         "combine_grads",
-        (sds((tok + 16, width), BF), sds((tok, width), BF)),
+        (sds((tok, width + LANES), BF), sds((tok, width), BF)),
         (1,),
         [whole(a.shape) for a in (routes, packed, mixed, gain, cot)],
-        (whole((tok + 16, width)), whole((tok, width))),
+        (whole((tok, width + LANES)), whole((tok, width))),
         flops=2 * packed.shape[0] * 2 * tok * width,
         nbytes=8 * packed.shape[0] * width,
     )(routes, packed, mixed, gain, cot)
@@ -505,38 +507,38 @@
 N_BLOCKS = 11
 
 
-def gather_parts(blocks, first, last):
+def gather_rows(blocks):
     same_z, other_z, left_z, right_z = blocks[:4], blocks[4], blocks[5:8], blocks[8:]
-    cut = left_z[0].shape[1]
+    width, cut = other_z.shape[1] - LANES, left_z[0].shape[1]
     left, right = [], []
     for d in range(4):
-        left += [same_z[d][first:last, :cut]]
-        left += [left_z[d - 1][first:last, :] if d else other_z[first:last, :cut]]
-        right += [same_z[d][first:last, cut:]]
-        right += [right_z[d - 1][first:last, :] if d else other_z[first:last, cut:]]
-    return left, right
-
-
-def gather_rows(blocks):
-    left, right = gather_parts(blocks, 0, blocks[0].shape[0] - 16)
+        left += [same_z[d][:, :cut], left_z[d - 1][...] if d else other_z[:, :cut]]
+        right += [same_z[d][:, cut:width]]
+        right += [right_z[d - 1][:, : width - cut] if d else other_z[:, cut:width]]
     return jnp.concatenate(left, axis=0), jnp.concatenate(right, axis=0)
+
+
+def gather_gain(blocks):
+    total = jnp.zeros((blocks[0].shape[0], LANES), F32)
+    for block in blocks[:5] + blocks[8:]:
+        total = total + block[:, block.shape[1] - LANES :].astype(F32)
+    per = (blocks[0].shape[1] - LANES) // LANES
+    rows = []
+    for q in range(per):
+        high, middle, low = [total[p * per + q : p * per + q + 1, :] for p in range(3)]
+        rows.append(high + middle + low)
+    return jnp.concatenate(rows, axis=1)
 
 
 def weight_give_body(order, ctx_got, *refs):
     blocks, (give, gain_out) = refs[:N_BLOCKS], refs[N_BLOCKS:]
-    tok = ctx_got.shape[1]
     ctx = rows_of(ctx_got, order, range(8))
-    gains = gather_parts(blocks, tok, tok + 16)
     first = 0
-    for h, rows in enumerate(gather_rows(blocks)):
+    for rows in gather_rows(blocks):
         last = first + rows.shape[1]
         give[:, first:last] = mm(ctx, rows, 0, 0).astype(BF)
-        total = jnp.zeros((16, last - first), F32)
-        for part in gains[h]:
-            total = total + part.astype(F32)
-        total = jnp.sum(total, axis=0, keepdims=True)
-        gain_out[:, first:last] = jnp.broadcast_to(total, (8, last - first))
         first = last
+    gain_out[...] = jnp.broadcast_to(gather_gain(blocks), gain_out.shape)
 
 
 def context_grad_body(order, w_own, w_got, *refs):

time: 335 us -> 333 us (level)
  transfers between devices with their start and end apart: 29 -> 29, of which waited for: 15 -> 15; matrix products, arithmetic and copies ran while one was open for 5% -> 5% of each run, Pallas kernels for 10% -> 9%
where the time goes in v1:
time: 333 us
  waiting for transfers between devices  96.1 us (29%)
  blocking collectives  81.9 us (25%)
  Pallas kernels  65.8 us (20%)
  starting transfers between devices  60.7 us (18%)
  local copies, waits for them, and re-layouts  11.3 us (3%)
  matrix products  11.1 us (3%)
  other arithmetic  4.66 us (1%)
    all_to_all x1, blocking collectives, trade(): lax.all_to_all(shaped, ('ctx', 'tp'), split_axis=0, concat_axis=0, tiled=...  81.9 us
    ppermute x23, waiting for transfers between devices, move(): return lax.ppermute(values, 'tp', perm)  52.6 us
    ppermute x23, starting transfers between devices, move(): return lax.ppermute(values, 'tp', perm)  40.1 us
    pallas_call x1, Pallas kernels, expert_call(): call(expert_body, 'expert', (sds((real * steps, width), BF), sds((real *...  24.7 us
    ppermute x3, waiting for transfers between devices, on_device(): over_y.append(lax.ppermute(sent[d], 'ctx', around))  21.8 us
    all_to_all x2, waiting for transfers between devices, trade(): lax.all_to_all(shaped, ('ctx', 'tp'), split_axis=0, concat_axis=0, tiled=...  21.8 us
    pallas_call x6, Pallas kernels, plain(): call(body, name, tuple(outs), (1,), [pl.BlockSpec(memory_space=pltpu.SMEM...  21.5 us
    all_to_all x2, starting transfers between devices, trade(): lax.all_to_all(shaped, ('ctx', 'tp'), split_axis=0, concat_axis=0, tiled=...  12.9 us
  transfers between devices with their start and end apart: 29, of which 15 were waited for; matrix products, arithmetic and copies ran while one was open for 5% of the time, Pallas kernels for 9%

profile of v1, /device:TPU:2, one launch (start us, length us, event | category | flops | bytes accessed | tf_op | source)
XLA Modules:
  0.0 332.6 jit_solution(5942325397534174423)
XLA Ops:
  1.3 2.3 collective-permute-done.ctx_got
  3.6 1.5 collective-permute-done.1.w_got
  7.5 2.1 project_first.1
  9.6 4.0 %collective-permute-start.2 = (bf16[512,1024]{1,0:T(8,128)(2,1)S(1)}, bf16[512,1024]{1,0:T(8,128)(2,1)S(1)}, u32[]{:S(2)}, u32[]{:S(2)}) collective-permute-start(bf16[512,1024]{1,0:T(8,128)(2,1)S(1)} %get-tuple-element.56), channel_id=1, source_target_pairs={{0,2},{1,3},{2,0},{3,1},{4,6},{5,7},{6,4},{7,5},{8,10},{9,11},{10,... | collective-permute-start | bytes 3145736 | tf_op jit(solution)/shard_map/ppermute | solution.py:616
  13.6 1.5 collective-permute-start.3
  16.2 2.2 collective-permute-start.5
  18.3 1.5 project_keep.1
  19.9 8.5 %collective-permute-done.3.got_1 = bf16[256,1024]{1,0:T(8,128)(2,1)S(1)} collective-permute-done((bf16[256,1024]{1,0:T(8,128)(2,1)S(1)}, bf16[256,1024]{1,0:T(8,128)(2,1)S(1)}, u32[]{:S(2)}, u32[]{:S(2)}) %collective-permute-start.3) | collective-permute-done | bytes 524320 | tf_op jit(solution)/shard_map/ppermute | solution.py:616
  28.4 3.0 collective-permute-done.4.got_2
  31.4 9.1 %collective-permute-done.5.got_3 = bf16[256,1024]{1,0:T(8,128)(2,1)S(1)} collective-permute-done((bf16[256,1024]{1,0:T(8,128)(2,1)S(1)}, bf16[256,1024]{1,0:T(8,128)(2,1)S(1)}, u32[]{:S(2)}, u32[]{:S(2)}) %collective-permute-start.5) | collective-permute-done | bytes 524320 | tf_op jit(solution)/shard_map/ppermute | solution.py:616
  40.5 1.6 add.203
  42.2 1.3 collective-permute-start.6
  43.5 1.5 collective-permute-start.7
  44.9 1.7 collective-permute-start.8
  47.2 2.6 pack_grads.1.refs_6_
  49.8 1.8 collective-permute-done.6.refs_0_
  51.6 2.8 collective-permute-done.7.refs_1_
  54.4 3.0 collective-permute-done.8.refs_2_
  57.4 3.3 norm_pack.1
  60.7 81.9 %all_to_all.15 = bf16[128,8,3072]{2,1,0:T(8,128)(2,1)} all-to-all(bf16[128,8,3072]{2,1,0:T(8,128)(2,1)S(1)} %bitcast.42), channel_id=1, replica_groups=mesh['ctx'=8,'tp'=16] {'ctx','tp'}, dimensions={0} | all-to-all | bytes 12582912 | tf_op jit(solution)/shard_map/all_to_all | solution.py:587
  142.6 24.7 %expert.1 = (bf16[768,2048]{1,0:T(8,128)(2,1)}, bf16[768,2048]{1,0:T(8,128)(2,1)}, bf16[768,768]{1,0:T(8,128)(2,1)}, bf16[768,1536]{1,0:T(8,128)(2,1)}, bf16[1024,1536]{1,0:T(8,128)(2,1)}) custom-call(bf16[1024,3072]{1,0:T(8,128)(2,1)} %bitcast.48, bf16[1024,3072]{1,0:T(8,128)(2,1)} %bitcast.49, bf16[2048,1536]{1,0:T(8,128)(2,1)} %bitcast.54, ...), custom_call_target="tpu_custom_call" | custom-call | flops 12079595520 | bytes 22020096 | tf_op jit(solution)/shard_map/expert/pallas_call | solution.py:397
  167.3 6.5 %all-to-all-start.1 = ((bf16[128,8,1536]{2,1,0:T(8,128)(2,1)}), bf16[128,8,1536]{2,1,0:T(8,128)(2,1)S(1)}, u32[]{:S(2)}, u32[]{:S(2)}) async-start(bf16[128,8,1536]{2,1,0:T(8,128)(2,1)} %bitcast.51), calls=%async_computation.1 | async-start | bytes 6291456 | tf_op jit(solution)/shard_map/all_to_all | solution.py:587
  173.9 7.9 %expert_y.1 = bf16[1024,1536]{1,0:T(8,128)(2,1)} custom-call(bf16[768,768]{1,0:T(8,128)(2,1)} %get-tuple-element.68.act, bf16[768,2048]{1,0:T(8,128)(2,1)} %bitcast.56), custom_call_target="tpu_custom_call" | custom-call | flops 2415919104 | bytes 9437184 | tf_op jit(solution)/shard_map/expert_y/pallas_call | solution.py:437
  181.8 4.0 %fusion.1 = bf16[1,768,2048]{2,1,0:T(8,128)(2,1)} fusion(bf16[768,768]{1,0:T(8,128)(2,1)S(1)} %copy-done.24, bf16[768,2048]{1,0:T(8,128)(2,1)S(1)} %copy-done.25), kind=kOutput, calls=%fused_computation.3 | convolution fusion | flops 2417491968 | bytes 7471104 | tf_op jit(solution)/shard_map/dot_general | solution.py:21
  185.8 7.1 %fusion = bf16[1,2048,1536]{2,1,0:T(8,128)(2,1)} fusion(bf16[768,2048]{1,0:T(8,128)(2,1)S(1)} %copy-done.26, bf16[768,1536]{1,0:T(8,128)(2,1)S(1)} %copy-done.27), kind=kOutput, calls=%fused_computation.1 | convolution fusion | flops 4834983936 | bytes 11796480 | tf_op jit(solution)/shard_map/dot_general | solution.py:21
  192.9 21.8 %all-to-all-done.1 = bf16[128,8,1536]{2,1,0:T(8,128)(2,1)S(1)} async-done(((bf16[128,8,1536]{2,1,0:T(8,128)(2,1)}), bf16[128,8,1536]{2,1,0:T(8,128)(2,1)S(1)}, u32[]{:S(2)}, u32[]{:S(2)}) %all-to-all-start.1) | async-done | bytes 3145760 | tf_op jit(solution)/shard_map/all_to_all | solution.py:587
  216.7 2.6 combine_grads.1
  219.3 1.2 collective-permute-start.10
  220.8 3.5 %collective-permute-start.11 = (bf16[128,2176]{1,0:T(8,128)(2,1)S(1)}, bf16[128,2176]{1,0:T(8,128)(2,1)S(1)}, u32[]{:S(2)}, u32[]{:S(2)}) collective-permute-start(bf16[128,2176]{1,0:T(8,128)(2,1)S(1)} %get-tuple-element.77.refs_0_), channel_id=1, source_target_pairs={{0,8},{1,9},{2,10},{3,11},{4,12},{5,13},{6,14},{7,15},{8,0},{9,1},... | collective-permute-start | bytes 1671176 | tf_op jit(solution)/shard_map/ppermute | solution.py:616
  224.4 10.5 %collective-permute-done.10.refs_1_ = bf16[128,2176]{1,0:T(8,128)(2,1)S(1)} collective-permute-done((bf16[128,2176]{1,0:T(8,128)(2,1)S(1)}, bf16[128,2176]{1,0:T(8,128)(2,1)S(1)}, u32[]{:S(2)}, u32[]{:S(2)}) %collective-permute-start.10) | collective-permute-done | bytes 557088 | tf_op jit(solution)/shard_map/ppermute | solution.py:616
  236.9 15.1 %collective-permute-start.18 = (bf16[128,1408]{1,0:T(8,128)(2,1)S(1)}, bf16[128,1408]{1,0:T(8,128)(2,1)}, u32[]{:S(2)}, u32[]{:S(2)}) collective-permute-start(bf16[128,1408]{1,0:T(8,128)(2,1)S(1)} %slice.38), channel_id=1, source_target_pairs={{0,8},{1,9},{2,10},{3,11},{4,12},{5,13},{6,14},{7,15},{8,0},{9,1},... | collective-permute-start | bytes 1081352 | tf_op jit(solution)/shard_map/ppermute | solution.py:616
  252.0 1.3 collective-permute-start.15
  253.4 2.4 collective-permute-start.16
  255.7 4.5 %collective-permute-done.15.refs_6_ = bf16[128,768]{1,0:T(8,128)(2,1)} collective-permute-done((bf16[128,768]{1,0:T(8,128)(2,1)S(1)}, bf16[128,768]{1,0:T(8,128)(2,1)}, u32[]{:S(2)}, u32[]{:S(2)}) %collective-permute-start.15) | collective-permute-done | bytes 196640 | tf_op jit(solution)/shard_map/ppermute | solution.py:616
  260.2 2.1 collective-permute-done.16.refs_7_
  262.3 2.6 collective-permute-done.19.refs_10_
  265.0 6.4 %all-to-all-start.2 = ((bf16[128,8,1536]{2,1,0:T(8,128)(2,1)}), bf16[128,8,1536]{2,1,0:T(8,128)(2,1)S(1)}, u32[]{:S(2)}, u32[]{:S(2)}) async-start(bf16[128,8,1536]{2,1,0:T(8,128)(2,1)} %bitcast.50), calls=%async_computation.2 | async-start | bytes 6291456 | tf_op jit(solution)/shard_map/all_to_all | solution.py:587
  272.1 4.8 %weight_give.1 = (bf16[256,2048]{1,0:T(8,128)(2,1)}, f32[8,2048]{1,0:T(8,128)}) custom-call(s32[8]{0:T(128)} %stack.65.order, bf16[16,128,256]{2,1,0:T(8,128)(2,1)} %copy-done.1, bf16[128,2176]{1,0:T(8,128)(2,1)} %copy-done.2, bf16[128,2176]{1,0:T(8,128)(2,1)} %copy-done.12, bf16[128,2176]{1,0:T(8,128)(2,1)} %copy-done.13, bf16[128,2176]{1,0:T(8,128)(2,1)} %copy-done.14, ...), custom_call_target="tpu_custom_call" | custom-call | flops 1073741824 | bytes 6619136 | tf_op jit(solution)/shard_map/weight_give/pallas_call | solution.py:494
  277.4 6.2 %context_grad.1 = (bf16[8,128,256]{2,1,0:T(8,128)(2,1)}, bf16[8,128,256]{2,1,0:T(8,128)(2,1)}) custom-call(s32[8]{0:T(128)} %stack.65.order, bf16[256,2048]{1,0:T(8,128)(2,1)} %w_own.5, bf16[256,2048]{1,0:T(8,128)(2,1)} %copy-done.4, bf16[128,2176]{1,0:T(8,128)(2,1)} %copy-done.2, bf16[128,2176]{1,0:T(8,128)(2,1)} %copy-done.12, ...), custom_call_target="tpu_custom_call" | custom-call | flops 2147483648 | bytes 7602176 | tf_op jit(solution)/shard_map/context_grad/pallas_call | solution.py:494
  286.2 5.2 %weight_own.1 = (bf16[2,288,256]{2,1,0:T(8,128)(2,1)}, bf16[2,288,256]{2,1,0:T(8,128)(2,1)}, bf16[2,288,256]{2,1,0:T(8,128)(2,1)}, bf16[2,288,256]{2,1,0:T(8,128)(2,1)}) custom-call(s32[9]{0:T(128)} %concatenate.10.order, bf16[16,128,256]{2,1,0:T(8,128)(2,1)} %bitcast.44, bf16[256,2048]{1,0:T(8,128)(2,1)} %collective-permute-done.20.got, ...), custom_call_target="tpu_custom_call" | custom-call | flops 1073741824 | bytes 7864320 | tf_op jit(solution)/shard_map/weight_own/pallas_call | solution.py:494
  291.4 1.5 collective-permute-start.22
  292.9 2.7 collective-permute-start.23
  295.7 1.4 collective-permute-start.24
  297.1 1.8 maximum_select_fusion
  299.9 21.8 %collective-permute-done.22 = bf16[2,288,256]{2,1,0:T(8,128)(2,1)} collective-permute-done((bf16[2,288,256]{2,1,0:T(8,128)(2,1)}, bf16[2,288,256]{2,1,0:T(8,128)(2,1)}, u32[]{:S(2)}, u32[]{:S(2)}) %collective-permute-start.22) | collective-permute-done | bytes 294944 | tf_op jit(solution)/shard_map/ppermute | solution.py:721
  321.7 1.3 convert_add_fusion
  323.9 2.1 collective-permute-start.25
  327.0 3.3 combine_out.1
  (100 shorter events, 18.3 us)
Async XLA Ops:
  0.6 3.0 collective-permute-start
  0.7 4.4 %collective-permute-start.1 = (bf16[256,2048]{1,0:T(8,128)(2,1)}, bf16[256,2048]{1,0:T(8,128)(2,1)S(1)}, u32[]{:S(2)}, u32[]{:S(2)}) collective-permute-start(bf16[256,2048]{1,0:T(8,128)(2,1)} %w_own.5), channel_id=1, source_target_pairs={{0,1},{1,0},{2,3},{3,2},{4,5},{5,4},{6,7},{7,6},{8,9},{9,8},{10,11... | collective-permute-start | bytes 3145736 | tf_op jit(solution)/shard_map/ppermute | solution.py:616
  3.6 16.3 %copy-start.1 = (bf16[16,128,256]{2,1,0:T(8,128)(2,1)}, bf16[16,128,256]{2,1,0:T(8,128)(2,1)S(1)}, u32[]{:S(2)}) copy-start(bf16[16,128,256]{2,1,0:T(8,128)(2,1)S(1)} %collective-permute-done.ctx_got) | copy-start | bytes 3145732
  7.5 12.3 %copy-start.4 = (bf16[256,2048]{1,0:T(8,128)(2,1)}, bf16[256,2048]{1,0:T(8,128)(2,1)S(1)}, u32[]{:S(2)}) copy-start(bf16[256,2048]{1,0:T(8,128)(2,1)S(1)} %collective-permute-done.1.w_got) | copy-start | bytes 3145732
  9.6 30.9 %collective-permute-start.2 = (bf16[512,1024]{1,0:T(8,128)(2,1)S(1)}, bf16[512,1024]{1,0:T(8,128)(2,1)S(1)}, u32[]{:S(2)}, u32[]{:S(2)}) collective-permute-start(bf16[512,1024]{1,0:T(8,128)(2,1)S(1)} %get-tuple-element.56), channel_id=1, source_target_pairs={{0,2},{1,3},{2,0},{3,1},{4,6},{5,7},{6,4},{7,5},{8,10},{9,11},{10,... | collective-permute-start | bytes 3145736 | tf_op jit(solution)/shard_map/ppermute | solution.py:616
  13.6 14.8 %collective-permute-start.3 = (bf16[256,1024]{1,0:T(8,128)(2,1)S(1)}, bf16[256,1024]{1,0:T(8,128)(2,1)S(1)}, u32[]{:S(2)}, u32[]{:S(2)}) collective-permute-start(bf16[256,1024]{1,0:T(8,128)(2,1)S(1)} %get-tuple-element.57), channel_id=1, source_target_pairs={{0,4},{1,5},{2,6},{3,7},{4,8},{5,9},{6,10},{7,11},{8,12},{9,13},{1... | collective-permute-start | bytes 1572872 | tf_op jit(solution)/shard_map/ppermute | solution.py:616
  15.1 16.4 %collective-permute-start.4 = (bf16[256,1024]{1,0:T(8,128)(2,1)S(1)}, bf16[256,1024]{1,0:T(8,128)(2,1)S(1)}, u32[]{:S(2)}, u32[]{:S(2)}) collective-permute-start(bf16[256,1024]{1,0:T(8,128)(2,1)S(1)} %get-tuple-element.58), channel_id=1, source_target_pairs={{0,8},{1,9},{2,10},{3,11},{4,12},{5,13},{6,14},{7,15},{8,0},{9,1},... | collective-permute-start | bytes 1572872 | tf_op jit(solution)/shard_map/ppermute | solution.py:616
  16.2 24.4 %collective-permute-start.5 = (bf16[256,1024]{1,0:T(8,128)(2,1)S(1)}, bf16[256,1024]{1,0:T(8,128)(2,1)S(1)}, u32[]{:S(2)}, u32[]{:S(2)}) collective-permute-start(bf16[256,1024]{1,0:T(8,128)(2,1)S(1)} %get-tuple-element.59), channel_id=1, source_target_pairs={{0,12},{1,13},{2,14},{3,15},{4,0},{5,1},{6,2},{7,3},{8,4},{9,5},{1... | collective-permute-start | bytes 1572872 | tf_op jit(solution)/shard_map/ppermute | solution.py:616
  19.9 27.1 %copy-start.22 = (s32[128,4]{0,1:T(4,128)S(1)}, s32[128,4]{0,1:T(4,128)}, u32[]{:S(2)}) copy-start(s32[128,4]{0,1:T(4,128)} %param.13) | copy-start | bytes 6148
  19.9 27.2 %copy-start.23 = (f32[128,4]{0,1:T(4,128)S(1)}, f32[128,4]{0,1:T(4,128)}, u32[]{:S(2)}) copy-start(f32[128,4]{0,1:T(4,128)} %param.14) | copy-start | bytes 6148
  19.9 27.3 %copy-start.21 = (bf16[2048]{0:T(1024)(128)(2,1)S(1)}, bf16[2048]{0:T(1024)(128)(2,1)}, u32[]{:S(2)}) copy-start(bf16[2048]{0:T(1024)(128)(2,1)} %param.12) | copy-start | bytes 12292
  19.9 27.3 %copy-start.6 = (bf16[128,2048]{1,0:T(8,128)(2,1)S(1)}, bf16[128,2048]{1,0:T(8,128)(2,1)}, u32[]{:S(2)}) copy-start(bf16[128,2048]{1,0:T(8,128)(2,1)} %cot.3) | copy-start | bytes 1572868
  42.2 15.3 %copy-start.5 = (bf16[128,2048]{1,0:T(8,128)(2,1)S(1)}, bf16[128,2048]{1,0:T(8,128)(2,1)}, u32[]{:S(2)}) copy-start(bf16[128,2048]{1,0:T(8,128)(2,1)} %refs_4_.1) | copy-start | bytes 1572868
  42.2 9.5 %collective-permute-start.6 = (bf16[128,1024]{1,0:T(8,128)(2,1)}, bf16[128,1024]{1,0:T(8,128)(2,1)S(1)}, u32[]{:S(2)}, u32[]{:S(2)}) collective-permute-start(bf16[128,1024]{1,0:T(8,128)(2,1)} %get-tuple-element.62), channel_id=1, source_target_pairs={{0,4},{1,5},{2,6},{3,7},{4,8},{5,9},{6,10},{7,11},{8,12},{9,13},{1... | collective-permute-start | bytes 786440 | tf_op jit(solution)/shard_map/ppermute | solution.py:616
  43.5 11.0 %collective-permute-start.7 = (bf16[128,1024]{1,0:T(8,128)(2,1)}, bf16[128,1024]{1,0:T(8,128)(2,1)S(1)}, u32[]{:S(2)}, u32[]{:S(2)}) collective-permute-start(bf16[128,1024]{1,0:T(8,128)(2,1)} %get-tuple-element.63), channel_id=1, source_target_pairs={{0,8},{1,9},{2,10},{3,11},{4,12},{5,13},{6,14},{7,15},{8,0},{9,1},... | collective-permute-start | bytes 786440 | tf_op jit(solution)/shard_map/ppermute | solution.py:616
  44.9 12.5 %collective-permute-start.8 = (bf16[128,1024]{1,0:T(8,128)(2,1)}, bf16[128,1024]{1,0:T(8,128)(2,1)S(1)}, u32[]{:S(2)}, u32[]{:S(2)}) collective-permute-start(bf16[128,1024]{1,0:T(8,128)(2,1)} %get-tuple-element.64), channel_id=1, source_target_pairs={{0,12},{1,13},{2,14},{3,15},{4,0},{5,1},{6,2},{7,3},{8,4},{9,5},{1... | collective-permute-start | bytes 786440 | tf_op jit(solution)/shard_map/ppermute | solution.py:616
  46.6 10.8 %collective-permute-start.9 = (bf16[128,1024]{1,0:T(8,128)(2,1)S(1)}, bf16[128,1024]{1,0:T(8,128)(2,1)S(1)}, u32[]{:S(2)}, u32[]{:S(2)}) collective-permute-start(bf16[128,1024]{1,0:T(8,128)(2,1)S(1)} %get-tuple-element.65), channel_id=1, source_target_pairs={{0,2},{1,3},{2,0},{3,1},{4,6},{5,7},{6,4},{7,5},{8,10},{9,11},{10,... | collective-permute-start | bytes 786440 | tf_op jit(solution)/shard_map/ppermute | solution.py:616
  60.7 81.9 %copy-start.8 = (bf16[128,2048]{1,0:T(8,128)(2,1)}, bf16[128,2048]{1,0:T(8,128)(2,1)S(1)}, u32[]{:S(2)}) copy-start(bf16[128,2048]{1,0:T(8,128)(2,1)S(1)} %get-tuple-element.74.mixed_ref.mixed) | copy-start | bytes 1572868
  167.3 47.3 %all-to-all-start.1 = ((bf16[128,8,1536]{2,1,0:T(8,128)(2,1)}), bf16[128,8,1536]{2,1,0:T(8,128)(2,1)S(1)}, u32[]{:S(2)}, u32[]{:S(2)}) async-start(bf16[128,8,1536]{2,1,0:T(8,128)(2,1)} %bitcast.51), calls=%async_computation.1 | async-start | bytes 6291456 | tf_op jit(solution)/shard_map/all_to_all | solution.py:587
  173.9 7.9 %copy-start.24 = (bf16[768,768]{1,0:T(8,128)(2,1)S(1)}, bf16[768,768]{1,0:T(8,128)(2,1)}, u32[]{:S(2)}) copy-start(bf16[768,768]{1,0:T(8,128)(2,1)} %get-tuple-element.68.act) | copy-start | bytes 3538948
  173.9 7.9 %copy-start.25 = (bf16[768,2048]{1,0:T(8,128)(2,1)S(1)}, bf16[768,2048]{1,0:T(8,128)(2,1)}, u32[]{:S(2)}) copy-start(bf16[768,2048]{1,0:T(8,128)(2,1)} %get-tuple-element.69) | copy-start | bytes 9437188
  181.8 4.0 %copy-start.26 = (bf16[768,2048]{1,0:T(8,128)(2,1)S(1)}, bf16[768,2048]{1,0:T(8,128)(2,1)}, u32[]{:S(2)}) copy-start(bf16[768,2048]{1,0:T(8,128)(2,1)} %get-tuple-element.70) | copy-start | bytes 9437188
  181.8 4.0 %copy-start.27 = (bf16[768,1536]{1,0:T(8,128)(2,1)S(1)}, bf16[768,1536]{1,0:T(8,128)(2,1)}, u32[]{:S(2)}) copy-start(bf16[768,1536]{1,0:T(8,128)(2,1)} %get-tuple-element.71) | copy-start | bytes 7077892
  219.3 5.0 %copy-start.2 = (bf16[128,2176]{1,0:T(8,128)(2,1)}, bf16[128,2176]{1,0:T(8,128)(2,1)S(1)}, u32[]{:S(2)}) copy-start(bf16[128,2176]{1,0:T(8,128)(2,1)S(1)} %get-tuple-element.77.refs_0_) | copy-start | bytes 1671172
  219.3 15.6 %collective-permute-start.10 = (bf16[128,2176]{1,0:T(8,128)(2,1)S(1)}, bf16[128,2176]{1,0:T(8,128)(2,1)S(1)}, u32[]{:S(2)}, u32[]{:S(2)}) collective-permute-start(bf16[128,2176]{1,0:T(8,128)(2,1)S(1)} %get-tuple-element.77.refs_0_), channel_id=1, source_target_pairs={{0,4},{1,5},{2,6},{3,7},{4,8},{5,9},{6,10},{7,11},{8,12},{9,13},{1... | collective-permute-start | bytes 1671176 | tf_op jit(solution)/shard_map/ppermute | solution.py:616
  220.6 16.1 %collective-permute-start.13 = (bf16[128,2176]{1,0:T(8,128)(2,1)S(1)}, bf16[128,2176]{1,0:T(8,128)(2,1)S(1)}, u32[]{:S(2)}, u32[]{:S(2)}) collective-permute-start(bf16[128,2176]{1,0:T(8,128)(2,1)S(1)} %get-tuple-element.77.refs_0_), channel_id=1, source_target_pairs={{0,2},{1,3},{2,0},{3,1},{4,6},{5,7},{6,4},{7,5},{8,10},{9,11},{10,... | collective-permute-start | bytes 1671176 | tf_op jit(solution)/shard_map/ppermute | solution.py:616
  220.8 31.1 %collective-permute-start.11 = (bf16[128,2176]{1,0:T(8,128)(2,1)S(1)}, bf16[128,2176]{1,0:T(8,128)(2,1)S(1)}, u32[]{:S(2)}, u32[]{:S(2)}) collective-permute-start(bf16[128,2176]{1,0:T(8,128)(2,1)S(1)} %get-tuple-element.77.refs_0_), channel_id=1, source_target_pairs={{0,8},{1,9},{2,10},{3,11},{4,12},{5,13},{6,14},{7,15},{8,0},{9,1},... | collective-permute-start | bytes 1671176 | tf_op jit(solution)/shard_map/ppermute | solution.py:616
  224.3 27.7 %collective-permute-start.12 = (bf16[128,2176]{1,0:T(8,128)(2,1)S(1)}, bf16[128,2176]{1,0:T(8,128)(2,1)S(1)}, u32[]{:S(2)}, u32[]{:S(2)}) collective-permute-start(bf16[128,2176]{1,0:T(8,128)(2,1)S(1)} %get-tuple-element.77.refs_0_), channel_id=1, source_target_pairs={{0,12},{1,13},{2,14},{3,15},{4,0},{5,1},{6,2},{7,3},{8,4},{9,5},{1... | collective-permute-start | bytes 1671176 | tf_op jit(solution)/shard_map/ppermute | solution.py:616
  235.7 17.6 %collective-permute-start.14 = (bf16[128,768]{1,0:T(8,128)(2,1)S(1)}, bf16[128,768]{1,0:T(8,128)(2,1)S(1)}, u32[]{:S(2)}, u32[]{:S(2)}) collective-permute-start(bf16[128,768]{1,0:T(8,128)(2,1)S(1)} %slice.35), channel_id=1, source_target_pairs={{0,2},{1,3},{2,0},{3,1},{4,6},{5,7},{6,4},{7,5},{8,10},{9,11},{10,... | collective-permute-start | bytes 589832 | tf_op jit(solution)/shard_map/ppermute | solution.py:616
  236.7 15.3 %copy-start.11 = (bf16[128,2176]{1,0:T(8,128)(2,1)}, bf16[128,2176]{1,0:T(8,128)(2,1)S(1)}, u32[]{:S(2)}) copy-start(bf16[128,2176]{1,0:T(8,128)(2,1)S(1)} %collective-permute-done.13.refs_4_) | copy-start | bytes 1671172
  236.7 25.6 %collective-permute-start.17 = (bf16[128,1408]{1,0:T(8,128)(2,1)S(1)}, bf16[128,1408]{1,0:T(8,128)(2,1)}, u32[]{:S(2)}, u32[]{:S(2)}) collective-permute-start(bf16[128,1408]{1,0:T(8,128)(2,1)S(1)} %slice.38), channel_id=1, source_target_pairs={{0,4},{1,5},{2,6},{3,7},{4,8},{5,9},{6,10},{7,11},{8,12},{9,13},{1... | collective-permute-start | bytes 1081352 | tf_op jit(solution)/shard_map/ppermute | solution.py:616
  236.9 25.5 %collective-permute-start.18 = (bf16[128,1408]{1,0:T(8,128)(2,1)S(1)}, bf16[128,1408]{1,0:T(8,128)(2,1)}, u32[]{:S(2)}, u32[]{:S(2)}) collective-permute-start(bf16[128,1408]{1,0:T(8,128)(2,1)S(1)} %slice.38), channel_id=1, source_target_pairs={{0,8},{1,9},{2,10},{3,11},{4,12},{5,13},{6,14},{7,15},{8,0},{9,1},... | collective-permute-start | bytes 1081352 | tf_op jit(solution)/shard_map/ppermute | solution.py:616
  251.9 1.4 copy-start.13
  251.9 13.0 %collective-permute-start.19 = (bf16[128,1408]{1,0:T(8,128)(2,1)S(1)}, bf16[128,1408]{1,0:T(8,128)(2,1)}, u32[]{:S(2)}, u32[]{:S(2)}) collective-permute-start(bf16[128,1408]{1,0:T(8,128)(2,1)S(1)} %slice.38), channel_id=1, source_target_pairs={{0,12},{1,13},{2,14},{3,15},{4,0},{5,1},{6,2},{7,3},{8,4},{9,5},{1... | collective-permute-start | bytes 1081352 | tf_op jit(solution)/shard_map/ppermute | solution.py:616
  252.0 8.2 %collective-permute-start.15 = (bf16[128,768]{1,0:T(8,128)(2,1)S(1)}, bf16[128,768]{1,0:T(8,128)(2,1)}, u32[]{:S(2)}, u32[]{:S(2)}) collective-permute-start(bf16[128,768]{1,0:T(8,128)(2,1)S(1)} %slice.36), channel_id=1, source_target_pairs={{0,2},{1,3},{2,0},{3,1},{4,6},{5,7},{6,4},{7,5},{8,10},{9,11},{10,... | collective-permute-start | bytes 589832 | tf_op jit(solution)/shard_map/ppermute | solution.py:616
  253.3 11.6 %copy-start.17 = (bf16[128,768]{1,0:T(8,128)(2,1)}, bf16[128,768]{1,0:T(8,128)(2,1)S(1)}, u32[]{:S(2)}) copy-start(bf16[128,768]{1,0:T(8,128)(2,1)S(1)} %collective-permute-done.14.refs_5_) | copy-start | bytes 589828
  253.4 9.0 %collective-permute-start.16 = (bf16[128,768]{1,0:T(8,128)(2,1)S(1)}, bf16[128,768]{1,0:T(8,128)(2,1)}, u32[]{:S(2)}, u32[]{:S(2)}) collective-permute-start(bf16[128,768]{1,0:T(8,128)(2,1)S(1)} %slice.37), channel_id=1, source_target_pairs={{0,2},{1,3},{2,0},{3,1},{4,6},{5,7},{6,4},{7,5},{8,10},{9,11},{10,... | collective-permute-start | bytes 589832 | tf_op jit(solution)/shard_map/ppermute | solution.py:616
  265.0 61.0 %all-to-all-start.2 = ((bf16[128,8,1536]{2,1,0:T(8,128)(2,1)}), bf16[128,8,1536]{2,1,0:T(8,128)(2,1)S(1)}, u32[]{:S(2)}, u32[]{:S(2)}) async-start(bf16[128,8,1536]{2,1,0:T(8,128)(2,1)} %bitcast.50), calls=%async_computation.2 | async-start | bytes 6291456 | tf_op jit(solution)/shard_map/all_to_all | solution.py:587
  276.9 7.0 %copy-start.19 = (f32[8,2048]{1,0:T(8,128)S(1)}, f32[8,2048]{1,0:T(8,128)}, u32[]{:S(2)}) copy-start(f32[8,2048]{1,0:T(8,128)} %get-tuple-element.89.gain_own) | copy-start | bytes 196612
  276.9 8.7 %collective-permute-start.20 = (bf16[256,2048]{1,0:T(8,128)(2,1)}, bf16[256,2048]{1,0:T(8,128)(2,1)}, u32[]{:S(2)}, u32[]{:S(2)}) collective-permute-start(bf16[256,2048]{1,0:T(8,128)(2,1)} %get-tuple-element.88), channel_id=1, source_target_pairs={{0,1},{1,0},{2,3},{3,2},{4,5},{5,4},{6,7},{7,6},{8,9},{9,8},{10,11... | collective-permute-start | bytes 3145736 | tf_op jit(solution)/shard_map/ppermute | solution.py:616
  283.6 13.5 %collective-permute-start.26 = (bf16[8,128,256]{2,1,0:T(8,128)(2,1)}, bf16[8,128,256]{2,1,0:T(8,128)(2,1)}, u32[]{:S(2)}, u32[]{:S(2)}) collective-permute-start(bf16[8,128,256]{2,1,0:T(8,128)(2,1)} %get-tuple-element.96), channel_id=1, source_target_pairs={{0,1},{1,0},{2,3},{3,2},{4,5},{5,4},{6,7},{7,6},{8,9},{9,8},{10,11... | collective-permute-start | bytes 1572872 | tf_op jit(solution)/shard_map/ppermute | solution.py:616
  283.9 1.6 collective-permute-start.21
  291.4 30.3 %collective-permute-start.22 = (bf16[2,288,256]{2,1,0:T(8,128)(2,1)}, bf16[2,288,256]{2,1,0:T(8,128)(2,1)}, u32[]{:S(2)}, u32[]{:S(2)}) collective-permute-start(bf16[2,288,256]{2,1,0:T(8,128)(2,1)} %get-tuple-element.91), channel_id=1, source_target_pairs={{0,32},{16,48},{32,64},{48,80},{64,96},{80,112},{96,0},{112,16},{1... | collective-permute-start | bytes 884744 | tf_op jit(solution)/shard_map/ppermute | solution.py:721
  292.9 28.8 %collective-permute-start.23 = (bf16[2,288,256]{2,1,0:T(8,128)(2,1)}, bf16[2,288,256]{2,1,0:T(8,128)(2,1)}, u32[]{:S(2)}, u32[]{:S(2)}) collective-permute-start(bf16[2,288,256]{2,1,0:T(8,128)(2,1)} %get-tuple-element.92), channel_id=1, source_target_pairs={{0,64},{16,80},{32,96},{48,112},{64,0},{80,16},{96,32},{112,48},{1... | collective-permute-start | bytes 884744 | tf_op jit(solution)/shard_map/ppermute | solution.py:721
  295.7 26.1 %collective-permute-start.24 = (bf16[2,288,256]{2,1,0:T(8,128)(2,1)}, bf16[2,288,256]{2,1,0:T(8,128)(2,1)}, u32[]{:S(2)}, u32[]{:S(2)}) collective-permute-start(bf16[2,288,256]{2,1,0:T(8,128)(2,1)} %get-tuple-element.93), channel_id=1, source_target_pairs={{0,96},{16,112},{32,0},{48,16},{64,32},{80,48},{96,64},{112,80},{1... | collective-permute-start | bytes 884744 | tf_op jit(solution)/shard_map/ppermute | solution.py:721
  297.1 24.7 %copy-start.18 = (bf16[2,288,256]{2,1,0:T(8,128)(2,1)S(1)}, bf16[2,288,256]{2,1,0:T(8,128)(2,1)}, u32[]{:S(2)}) copy-start(bf16[2,288,256]{2,1,0:T(8,128)(2,1)} %get-tuple-element.90) | copy-start | bytes 884740
  323.9 6.4 %collective-permute-start.25 = (bf16[288,256]{1,0:T(8,128)(2,1)S(1)}, bf16[288,256]{1,0:T(8,128)(2,1)}, u32[]{:S(2)}, u32[]{:S(2)}) collective-permute-start(bf16[288,256]{1,0:T(8,128)(2,1)S(1)} %fusion.3), channel_id=1, source_target_pairs={{0,16},{16,0},{32,48},{48,32},{64,80},{80,64},{96,112},{112,96},{1... | collective-permute-start | bytes 442376 | tf_op jit(solution)/shard_map/ppermute | solution.py:725
  327.0 3.3 copy-start.16
  (9 other events, 9.2 us)

commit v2 on v1

--- a/solution.py
+++ b/solution.py
@@ -559,9 +559,9 @@
     n_ctx, _, width = held.shape
     ctx = rows_of(ctx_own, order, range(8))
     parts = thirds(gain_own[0:1, :] + gain_got[0:1, :])
-    row = iota((32, width), 0)
-    gain = jnp.zeros((32, width), F32)
-    for p in range(3):
+    row = iota((16, width), 0)
+    gain = jnp.zeros((16, width), F32)
+    for p in range(2):
         for j in range(n_ctx):
             piece = parts[p][:, j * width : (j + 1) * width].astype(F32)
             gain = jnp.where(row == p * n_ctx + j, piece, gain)
@@ -573,7 +573,7 @@
         grad = grad.astype(BF)
         for j in range(first // width, last // width):
             held[j, 0:cols, :] = grad[:, j * width - first : (j + 1) * width - first]
-            held[j, cols : cols + 32, :] = gain
+            held[j, cols : cols + 16, :] = gain
         first = last
     y, z = order[8] // 2, order[8] % 2
     for d, out in enumerate(outs):
@@ -690,7 +690,7 @@
     w_grad_got = move(w_give, swap)
     gain_got = move(gain_own, swap)
     out_cols = width // n_ctx
-    part = (cols + 32, out_cols)
+    part = (cols + 16, out_cols)
     sent = plain(
         weight_own_body,
         "weight_own",
@@ -720,13 +720,13 @@
         around = [(u, (u + 2 * d) % n_ctx) for u in range(n_ctx)]
         over_y.append(lax.ppermute(sent[d], "ctx", around))
     layer_out = combine_out(routes, gate_weights, y_back, mixed, n_exp)
+    layer_out, *over_y = lax.optimization_barrier((layer_out, *over_y))
     summed = sum(f.astype(F32) for f in over_y)
     other = summed[1].astype(BF)
     last = lax.ppermute(other, "ctx", [(u, u ^ 1) for u in range(n_ctx)])
-    layer_out, last = lax.optimization_barrier((layer_out, last))
     final = summed[0] + last.astype(F32)
     d_o_weight = final[:cols]
-    d_gain = jnp.sum(final[cols : cols + 3 * n_ctx].reshape(3, width), axis=0)
+    d_gain = jnp.sum(final[cols : cols + 2 * n_ctx].reshape(2, width), axis=0)
 
     mine = ctx_mine.reshape(chips, 1, tok, cols)
     other = ctx_other.reshape(chips, 1, tok, cols)

time: 333 us -> 330 us (level)
    ppermute x3, waiting for transfers between devices: 21.8 us -> 3.49 us  [on_device(): over_y.append(lax.ppermute(sent[d], 'ctx', around))]
    all_to_all x2, waiting for transfers between devices: 21.8 us -> 37.4 us  [trade(): lax.all_to_all(shaped, ('ctx', 'tp'), split_axis=0, concat_axis=0, tiled=...]
    unnamed x58 -> x52, local copies, waits for them, and re-layouts: 8.11 us -> 7.27 us
  transfers between devices with their start and end apart: 29 -> 29, of which waited for: 15 -> 17; matrix products, arithmetic and copies ran while one was open for 5% -> 5% of each run, Pallas kernels for 9% -> 10%
where the time goes in v2:
time: 330 us; the launch traced here: 329 us
  waiting for transfers between devices  95.2 us (29%)
  blocking collectives  81.9 us (25%)
  Pallas kernels  65.9 us (20%)
  starting transfers between devices  60.2 us (18%)
  matrix products  11.1 us (3%)
  local copies, waits for them, and re-layouts  10.4 us (3%)
  other arithmetic  3.6 us (1%)
    all_to_all x1, blocking collectives, trade(): lax.all_to_all(shaped, ('ctx', 'tp'), split_axis=0, concat_axis=0, tiled=...  81.9 us
    ppermute x23, waiting for transfers between devices, move(): return lax.ppermute(values, 'tp', perm)  53.6 us
    ppermute x23, starting transfers between devices, move(): return lax.ppermute(values, 'tp', perm)  39.6 us
    all_to_all x2, waiting for transfers between devices, trade(): lax.all_to_all(shaped, ('ctx', 'tp'), split_axis=0, concat_axis=0, tiled=...  37.4 us
    pallas_call x1, Pallas kernels, expert_call(): call(expert_body, 'expert', (sds((real * steps, width), BF), sds((real *...  24.7 us
    pallas_call x6, Pallas kernels, plain(): call(body, name, tuple(outs), (1,), [pl.BlockSpec(memory_space=pltpu.SMEM...  21.5 us
    all_to_all x2, starting transfers between devices, trade(): lax.all_to_all(shaped, ('ctx', 'tp'), split_axis=0, concat_axis=0, tiled=...  12.9 us
    dot_general x2, matrix products, mm(): lax.dot_general(a, b, (((da,), (db,)), ((), ())), preferred_element_type=...  11.1 us
  transfers between devices with their start and end apart: 29, of which 17 were waited for; matrix products, arithmetic and copies ran while one was open for 5% of the time, Pallas kernels for 10%

profile of v2, /device:TPU:2, one launch (start us, length us, event | category | flops | bytes accessed | tf_op | source)
XLA Modules:
  0.0 329.4 jit_solution(17693817303026628892)
XLA Ops:
  1.3 2.3 collective-permute-done.ctx_got
  3.6 1.5 collective-permute-done.1.w_got
  7.5 2.1 project_first.1
  9.6 4.0 %collective-permute-start.2 = (bf16[512,1024]{1,0:T(8,128)(2,1)S(1)}, bf16[512,1024]{1,0:T(8,128)(2,1)S(1)}, u32[]{:S(2)}, u32[]{:S(2)}) collective-permute-start(bf16[512,1024]{1,0:T(8,128)(2,1)S(1)} %get-tuple-element.59), channel_id=1, source_target_pairs={{0,2},{1,3},{2,0},{3,1},{4,6},{5,7},{6,4},{7,5},{8,10},{9,11},{10,... | collective-permute-start | bytes 3145736 | tf_op jit(solution)/shard_map/ppermute | solution.py:616
  13.6 1.5 collective-permute-start.3
  16.2 2.2 collective-permute-start.5
  18.3 1.5 project_keep.1
  19.9 8.5 %collective-permute-done.3.got_1 = bf16[256,1024]{1,0:T(8,128)(2,1)S(1)} collective-permute-done((bf16[256,1024]{1,0:T(8,128)(2,1)S(1)}, bf16[256,1024]{1,0:T(8,128)(2,1)S(1)}, u32[]{:S(2)}, u32[]{:S(2)}) %collective-permute-start.3) | collective-permute-done | bytes 524320 | tf_op jit(solution)/shard_map/ppermute | solution.py:616
  28.4 3.0 collective-permute-done.4.got_2
  31.4 9.1 %collective-permute-done.5.got_3 = bf16[256,1024]{1,0:T(8,128)(2,1)S(1)} collective-permute-done((bf16[256,1024]{1,0:T(8,128)(2,1)S(1)}, bf16[256,1024]{1,0:T(8,128)(2,1)S(1)}, u32[]{:S(2)}, u32[]{:S(2)}) %collective-permute-start.5) | collective-permute-done | bytes 524320 | tf_op jit(solution)/shard_map/ppermute | solution.py:616
  40.5 1.6 add.203
  42.2 1.3 collective-permute-start.6
  43.5 1.5 collective-permute-start.7
  44.9 1.7 collective-permute-start.8
  47.2 2.6 pack_grads.1.refs_6_
  49.8 1.8 collective-permute-done.6.refs_0_
  51.6 2.8 collective-permute-done.7.refs_1_
  54.4 3.0 collective-permute-done.8.refs_2_
  57.4 3.3 norm_pack.1
  60.7 81.9 %all_to_all.15 = bf16[128,8,3072]{2,1,0:T(8,128)(2,1)} all-to-all(bf16[128,8,3072]{2,1,0:T(8,128)(2,1)S(1)} %bitcast.42), channel_id=1, replica_groups=mesh['ctx'=8,'tp'=16] {'ctx','tp'}, dimensions={0} | all-to-all | bytes 12582912 | tf_op jit(solution)/shard_map/all_to_all | solution.py:587
  142.6 24.7 %expert.1 = (bf16[768,2048]{1,0:T(8,128)(2,1)}, bf16[768,2048]{1,0:T(8,128)(2,1)}, bf16[768,768]{1,0:T(8,128)(2,1)}, bf16[768,1536]{1,0:T(8,128)(2,1)}, bf16[1024,1536]{1,0:T(8,128)(2,1)}) custom-call(bf16[1024,3072]{1,0:T(8,128)(2,1)} %bitcast.48, bf16[1024,3072]{1,0:T(8,128)(2,1)} %bitcast.49, bf16[2048,1536]{1,0:T(8,128)(2,1)} %bitcast.54, ...), custom_call_target="tpu_custom_call" | custom-call | flops 12079595520 | bytes 22020096 | tf_op jit(solution)/shard_map/expert/pallas_call | solution.py:397
  167.4 6.5 %all-to-all-start.1 = ((bf16[128,8,1536]{2,1,0:T(8,128)(2,1)}), bf16[128,8,1536]{2,1,0:T(8,128)(2,1)S(1)}, u32[]{:S(2)}, u32[]{:S(2)}) async-start(bf16[128,8,1536]{2,1,0:T(8,128)(2,1)} %bitcast.51), calls=%async_computation.1 | async-start | bytes 6291456 | tf_op jit(solution)/shard_map/all_to_all | solution.py:587
  173.9 7.9 %expert_y.1 = bf16[1024,1536]{1,0:T(8,128)(2,1)} custom-call(bf16[768,768]{1,0:T(8,128)(2,1)} %get-tuple-element.71.act, bf16[768,2048]{1,0:T(8,128)(2,1)} %bitcast.56), custom_call_target="tpu_custom_call" | custom-call | flops 2415919104 | bytes 9437184 | tf_op jit(solution)/shard_map/expert_y/pallas_call | solution.py:437
  181.8 4.0 %fusion.1 = bf16[1,768,2048]{2,1,0:T(8,128)(2,1)} fusion(bf16[768,768]{1,0:T(8,128)(2,1)S(1)} %copy-done.21, bf16[768,2048]{1,0:T(8,128)(2,1)S(1)} %copy-done.22), kind=kOutput, calls=%fused_computation.3 | convolution fusion | flops 2417491968 | bytes 7471104 | tf_op jit(solution)/shard_map/dot_general | solution.py:21
  185.9 7.1 %fusion = bf16[1,2048,1536]{2,1,0:T(8,128)(2,1)} fusion(bf16[768,2048]{1,0:T(8,128)(2,1)S(1)} %copy-done.23, bf16[768,1536]{1,0:T(8,128)(2,1)S(1)} %copy-done.24), kind=kOutput, calls=%fused_computation.1 | convolution fusion | flops 4834983936 | bytes 11796480 | tf_op jit(solution)/shard_map/dot_general | solution.py:21
  192.9 21.8 %all-to-all-done.1 = bf16[128,8,1536]{2,1,0:T(8,128)(2,1)S(1)} async-done(((bf16[128,8,1536]{2,1,0:T(8,128)(2,1)}), bf16[128,8,1536]{2,1,0:T(8,128)(2,1)S(1)}, u32[]{:S(2)}, u32[]{:S(2)}) %all-to-all-start.1) | async-done | bytes 3145760 | tf_op jit(solution)/shard_map/all_to_all | solution.py:587
  216.8 2.6 combine_grads.1
  220.8 3.5 %collective-permute-start.11 = (bf16[128,2176]{1,0:T(8,128)(2,1)S(1)}, bf16[128,2176]{1,0:T(8,128)(2,1)S(1)}, u32[]{:S(2)}, u32[]{:S(2)}) collective-permute-start(bf16[128,2176]{1,0:T(8,128)(2,1)S(1)} %get-tuple-element.80.refs_0_), channel_id=1, source_target_pairs={{0,8},{1,9},{2,10},{3,11},{4,12},{5,13},{6,14},{7,15},{8,0},{9,1},... | collective-permute-start | bytes 1671176 | tf_op jit(solution)/shard_map/ppermute | solution.py:616
  224.5 10.5 %collective-permute-done.10.refs_1_ = bf16[128,2176]{1,0:T(8,128)(2,1)S(1)} collective-permute-done((bf16[128,2176]{1,0:T(8,128)(2,1)S(1)}, bf16[128,2176]{1,0:T(8,128)(2,1)S(1)}, u32[]{:S(2)}, u32[]{:S(2)}) %collective-permute-start.10) | collective-permute-done | bytes 557088 | tf_op jit(solution)/shard_map/ppermute | solution.py:616
  236.9 15.1 %collective-permute-start.18 = (bf16[128,1408]{1,0:T(8,128)(2,1)S(1)}, bf16[128,1408]{1,0:T(8,128)(2,1)}, u32[]{:S(2)}, u32[]{:S(2)}) collective-permute-start(bf16[128,1408]{1,0:T(8,128)(2,1)S(1)} %slice.38), channel_id=1, source_target_pairs={{0,8},{1,9},{2,10},{3,11},{4,12},{5,13},{6,14},{7,15},{8,0},{9,1},... | collective-permute-start | bytes 1081352 | tf_op jit(solution)/shard_map/ppermute | solution.py:616
  252.0 1.3 collective-permute-start.15
  253.4 2.4 collective-permute-start.16
  255.8 4.5 %collective-permute-done.15.refs_6_ = bf16[128,768]{1,0:T(8,128)(2,1)} collective-permute-done((bf16[128,768]{1,0:T(8,128)(2,1)S(1)}, bf16[128,768]{1,0:T(8,128)(2,1)}, u32[]{:S(2)}, u32[]{:S(2)}) %collective-permute-start.15) | collective-permute-done | bytes 196640 | tf_op jit(solution)/shard_map/ppermute | solution.py:616
  260.2 2.1 collective-permute-done.16.refs_7_
  262.3 2.6 collective-permute-done.19.refs_10_
  265.0 6.4 %all-to-all-start.2 = ((bf16[128,8,1536]{2,1,0:T(8,128)(2,1)}), bf16[128,8,1536]{2,1,0:T(8,128)(2,1)S(1)}, u32[]{:S(2)}, u32[]{:S(2)}) async-start(bf16[128,8,1536]{2,1,0:T(8,128)(2,1)} %bitcast.50), calls=%async_computation.2 | async-start | bytes 6291456 | tf_op jit(solution)/shard_map/all_to_all | solution.py:587
  272.1 4.8 %weight_give.1 = (bf16[256,2048]{1,0:T(8,128)(2,1)}, f32[8,2048]{1,0:T(8,128)}) custom-call(s32[8]{0:T(128)} %stack.65.order, bf16[16,128,256]{2,1,0:T(8,128)(2,1)} %copy-done.1, bf16[128,2176]{1,0:T(8,128)(2,1)} %copy-done.2, bf16[128,2176]{1,0:T(8,128)(2,1)} %copy-done.12, bf16[128,2176]{1,0:T(8,128)(2,1)} %copy-done.13, bf16[128,2176]{1,0:T(8,128)(2,1)} %copy-done.14, ...), custom_call_target="tpu_custom_call" | custom-call | flops 1073741824 | bytes 6619136 | tf_op jit(solution)/shard_map/weight_give/pallas_call | solution.py:494
  278.0 1.8 collective-permute-done.21.gain_got
  280.5 5.3 %weight_own.1 = (bf16[2,272,256]{2,1,0:T(8,128)(2,1)}, bf16[2,272,256]{2,1,0:T(8,128)(2,1)}, bf16[2,272,256]{2,1,0:T(8,128)(2,1)}, bf16[2,272,256]{2,1,0:T(8,128)(2,1)}) custom-call(s32[9]{0:T(128)} %concatenate.10.order, bf16[16,128,256]{2,1,0:T(8,128)(2,1)} %bitcast.44, bf16[256,2048]{1,0:T(8,128)(2,1)} %collective-permute-done.20.got, ...), custom_call_target="tpu_custom_call" | custom-call | flops 1073741824 | bytes 7798784 | tf_op jit(solution)/shard_map/weight_own/pallas_call | solution.py:494
  285.7 1.5 collective-permute-start.22
  287.2 2.7 collective-permute-start.23
  289.9 1.4 collective-permute-start.24
  291.3 6.2 %context_grad.1 = (bf16[8,128,256]{2,1,0:T(8,128)(2,1)}, bf16[8,128,256]{2,1,0:T(8,128)(2,1)}) custom-call(s32[8]{0:T(128)} %stack.65.order, bf16[256,2048]{1,0:T(8,128)(2,1)} %w_own.5, bf16[256,2048]{1,0:T(8,128)(2,1)} %copy-done.4, bf16[128,2176]{1,0:T(8,128)(2,1)} %copy-done.2, bf16[128,2176]{1,0:T(8,128)(2,1)} %copy-done.12, ...), custom_call_target="tpu_custom_call" | custom-call | flops 2147483648 | bytes 7602176 | tf_op jit(solution)/shard_map/context_grad/pallas_call | solution.py:494
  297.5 15.7 %all-to-all-done.2 = bf16[128,8,1536]{2,1,0:T(8,128)(2,1)S(1)} async-done(((bf16[128,8,1536]{2,1,0:T(8,128)(2,1)}), bf16[128,8,1536]{2,1,0:T(8,128)(2,1)S(1)}, u32[]{:S(2)}, u32[]{:S(2)}) %all-to-all-start.2) | async-done | bytes 3145760 | tf_op jit(solution)/shard_map/all_to_all | solution.py:587
  314.3 3.3 %combine_out.1 = bf16[128,2048]{1,0:T(8,128)(2,1)} custom-call(s32[128,4]{1,0:T(8,128)S(1)} %copy.26.routes, f32[128,4]{1,0:T(8,128)S(1)} %copy.27.gates, bf16[1024,1536]{1,0:T(8,128)(2,1)S(1)} %bitcast.47, bf16[128,2048]{1,0:T(8,128)(2,1)S(1)} %copy-done.10), custom_call_target="tpu_custom_call" | custom-call | flops 2147483648 | bytes 12582912 | tf_op jit(solution)/shard_map/combine_out/pallas_call | solution.py:327
  317.6 3.5 %collective-permute-done.22 = bf16[2,272,256]{2,1,0:T(8,128)(2,1)} collective-permute-done((bf16[2,272,256]{2,1,0:T(8,128)(2,1)}, bf16[2,272,256]{2,1,0:T(8,128)(2,1)}, u32[]{:S(2)}, u32[]{:S(2)}) %collective-permute-start.22) | collective-permute-done | bytes 278560 | tf_op jit(solution)/shard_map/ppermute | solution.py:721
  322.3 2.1 collective-permute-start.26
  324.5 1.7 maximum_select_fusion
  (94 shorter events, 18.4 us)
Async XLA Ops:
  0.6 3.0 collective-permute-start
  0.7 4.4 %collective-permute-start.1 = (bf16[256,2048]{1,0:T(8,128)(2,1)}, bf16[256,2048]{1,0:T(8,128)(2,1)S(1)}, u32[]{:S(2)}, u32[]{:S(2)}) collective-permute-start(bf16[256,2048]{1,0:T(8,128)(2,1)} %w_own.5), channel_id=1, source_target_pairs={{0,1},{1,0},{2,3},{3,2},{4,5},{5,4},{6,7},{7,6},{8,9},{9,8},{10,11... | collective-permute-start | bytes 3145736 | tf_op jit(solution)/shard_map/ppermute | solution.py:616
  3.6 16.3 %copy-start.1 = (bf16[16,128,256]{2,1,0:T(8,128)(2,1)}, bf16[16,128,256]{2,1,0:T(8,128)(2,1)S(1)}, u32[]{:S(2)}) copy-start(bf16[16,128,256]{2,1,0:T(8,128)(2,1)S(1)} %collective-permute-done.ctx_got) | copy-start | bytes 3145732
  5.1 1.2 copy-start
  7.5 12.3 %copy-start.4 = (bf16[256,2048]{1,0:T(8,128)(2,1)}, bf16[256,2048]{1,0:T(8,128)(2,1)S(1)}, u32[]{:S(2)}) copy-start(bf16[256,2048]{1,0:T(8,128)(2,1)S(1)} %collective-permute-done.1.w_got) | copy-start | bytes 3145732
  9.6 30.9 %collective-permute-start.2 = (bf16[512,1024]{1,0:T(8,128)(2,1)S(1)}, bf16[512,1024]{1,0:T(8,128)(2,1)S(1)}, u32[]{:S(2)}, u32[]{:S(2)}) collective-permute-start(bf16[512,1024]{1,0:T(8,128)(2,1)S(1)} %get-tuple-element.59), channel_id=1, source_target_pairs={{0,2},{1,3},{2,0},{3,1},{4,6},{5,7},{6,4},{7,5},{8,10},{9,11},{10,... | collective-permute-start | bytes 3145736 | tf_op jit(solution)/shard_map/ppermute | solution.py:616
  13.6 14.8 %collective-permute-start.3 = (bf16[256,1024]{1,0:T(8,128)(2,1)S(1)}, bf16[256,1024]{1,0:T(8,128)(2,1)S(1)}, u32[]{:S(2)}, u32[]{:S(2)}) collective-permute-start(bf16[256,1024]{1,0:T(8,128)(2,1)S(1)} %get-tuple-element.60), channel_id=1, source_target_pairs={{0,4},{1,5},{2,6},{3,7},{4,8},{5,9},{6,10},{7,11},{8,12},{9,13},{1... | collective-permute-start | bytes 1572872 | tf_op jit(solution)/shard_map/ppermute | solution.py:616
  15.1 16.4 %collective-permute-start.4 = (bf16[256,1024]{1,0:T(8,128)(2,1)S(1)}, bf16[256,1024]{1,0:T(8,128)(2,1)S(1)}, u32[]{:S(2)}, u32[]{:S(2)}) collective-permute-start(bf16[256,1024]{1,0:T(8,128)(2,1)S(1)} %get-tuple-element.61), channel_id=1, source_target_pairs={{0,8},{1,9},{2,10},{3,11},{4,12},{5,13},{6,14},{7,15},{8,0},{9,1},... | collective-permute-start | bytes 1572872 | tf_op jit(solution)/shard_map/ppermute | solution.py:616
  16.2 24.4 %collective-permute-start.5 = (bf16[256,1024]{1,0:T(8,128)(2,1)S(1)}, bf16[256,1024]{1,0:T(8,128)(2,1)S(1)}, u32[]{:S(2)}, u32[]{:S(2)}) collective-permute-start(bf16[256,1024]{1,0:T(8,128)(2,1)S(1)} %get-tuple-element.62), channel_id=1, source_target_pairs={{0,12},{1,13},{2,14},{3,15},{4,0},{5,1},{6,2},{7,3},{8,4},{9,5},{1... | collective-permute-start | bytes 1572872 | tf_op jit(solution)/shard_map/ppermute | solution.py:616
  19.9 27.1 %copy-start.19 = (s32[128,4]{0,1:T(4,128)S(1)}, s32[128,4]{0,1:T(4,128)}, u32[]{:S(2)}) copy-start(s32[128,4]{0,1:T(4,128)} %param.13) | copy-start | bytes 6148
  19.9 27.2 %copy-start.20 = (f32[128,4]{0,1:T(4,128)S(1)}, f32[128,4]{0,1:T(4,128)}, u32[]{:S(2)}) copy-start(f32[128,4]{0,1:T(4,128)} %param.14) | copy-start | bytes 6148
  19.9 27.3 %copy-start.18 = (bf16[2048]{0:T(1024)(128)(2,1)S(1)}, bf16[2048]{0:T(1024)(128)(2,1)}, u32[]{:S(2)}) copy-start(bf16[2048]{0:T(1024)(128)(2,1)} %param.12) | copy-start | bytes 12292
  19.9 27.3 %copy-start.6 = (bf16[128,2048]{1,0:T(8,128)(2,1)S(1)}, bf16[128,2048]{1,0:T(8,128)(2,1)}, u32[]{:S(2)}) copy-start(bf16[128,2048]{1,0:T(8,128)(2,1)} %cot.3) | copy-start | bytes 1572868
  42.2 15.3 %copy-start.5 = (bf16[128,2048]{1,0:T(8,128)(2,1)S(1)}, bf16[128,2048]{1,0:T(8,128)(2,1)}, u32[]{:S(2)}) copy-start(bf16[128,2048]{1,0:T(8,128)(2,1)} %refs_4_.1) | copy-start | bytes 1572868
  42.2 9.5 %collective-permute-start.6 = (bf16[128,1024]{1,0:T(8,128)(2,1)}, bf16[128,1024]{1,0:T(8,128)(2,1)S(1)}, u32[]{:S(2)}, u32[]{:S(2)}) collective-permute-start(bf16[128,1024]{1,0:T(8,128)(2,1)} %get-tuple-element.65), channel_id=1, source_target_pairs={{0,4},{1,5},{2,6},{3,7},{4,8},{5,9},{6,10},{7,11},{8,12},{9,13},{1... | collective-permute-start | bytes 786440 | tf_op jit(solution)/shard_map/ppermute | solution.py:616
  43.5 11.0 %collective-permute-start.7 = (bf16[128,1024]{1,0:T(8,128)(2,1)}, bf16[128,1024]{1,0:T(8,128)(2,1)S(1)}, u32[]{:S(2)}, u32[]{:S(2)}) collective-permute-start(bf16[128,1024]{1,0:T(8,128)(2,1)} %get-tuple-element.66), channel_id=1, source_target_pairs={{0,8},{1,9},{2,10},{3,11},{4,12},{5,13},{6,14},{7,15},{8,0},{9,1},... | collective-permute-start | bytes 786440 | tf_op jit(solution)/shard_map/ppermute | solution.py:616
  44.9 12.5 %collective-permute-start.8 = (bf16[128,1024]{1,0:T(8,128)(2,1)}, bf16[128,1024]{1,0:T(8,128)(2,1)S(1)}, u32[]{:S(2)}, u32[]{:S(2)}) collective-permute-start(bf16[128,1024]{1,0:T(8,128)(2,1)} %get-tuple-element.67), channel_id=1, source_target_pairs={{0,12},{1,13},{2,14},{3,15},{4,0},{5,1},{6,2},{7,3},{8,4},{9,5},{1... | collective-permute-start | bytes 786440 | tf_op jit(solution)/shard_map/ppermute | solution.py:616
  46.6 10.8 %collective-permute-start.9 = (bf16[128,1024]{1,0:T(8,128)(2,1)S(1)}, bf16[128,1024]{1,0:T(8,128)(2,1)S(1)}, u32[]{:S(2)}, u32[]{:S(2)}) collective-permute-start(bf16[128,1024]{1,0:T(8,128)(2,1)S(1)} %get-tuple-element.68), channel_id=1, source_target_pairs={{0,2},{1,3},{2,0},{3,1},{4,6},{5,7},{6,4},{7,5},{8,10},{9,11},{10,... | collective-permute-start | bytes 786440 | tf_op jit(solution)/shard_map/ppermute | solution.py:616
  60.7 81.9 %copy-start.8 = (bf16[128,2048]{1,0:T(8,128)(2,1)}, bf16[128,2048]{1,0:T(8,128)(2,1)S(1)}, u32[]{:S(2)}) copy-start(bf16[128,2048]{1,0:T(8,128)(2,1)S(1)} %get-tuple-element.77.mixed_ref.mixed) | copy-start | bytes 1572868
  167.4 47.3 %all-to-all-start.1 = ((bf16[128,8,1536]{2,1,0:T(8,128)(2,1)}), bf16[128,8,1536]{2,1,0:T(8,128)(2,1)S(1)}, u32[]{:S(2)}, u32[]{:S(2)}) async-start(bf16[128,8,1536]{2,1,0:T(8,128)(2,1)} %bitcast.51), calls=%async_computation.1 | async-start | bytes 6291456 | tf_op jit(solution)/shard_map/all_to_all | solution.py:587
  173.9 7.9 %copy-start.21 = (bf16[768,768]{1,0:T(8,128)(2,1)S(1)}, bf16[768,768]{1,0:T(8,128)(2,1)}, u32[]{:S(2)}) copy-start(bf16[768,768]{1,0:T(8,128)(2,1)} %get-tuple-element.71.act) | copy-start | bytes 3538948
  173.9 7.9 %copy-start.22 = (bf16[768,2048]{1,0:T(8,128)(2,1)S(1)}, bf16[768,2048]{1,0:T(8,128)(2,1)}, u32[]{:S(2)}) copy-start(bf16[768,2048]{1,0:T(8,128)(2,1)} %get-tuple-element.72) | copy-start | bytes 9437188
  181.8 4.0 %copy-start.23 = (bf16[768,2048]{1,0:T(8,128)(2,1)S(1)}, bf16[768,2048]{1,0:T(8,128)(2,1)}, u32[]{:S(2)}) copy-start(bf16[768,2048]{1,0:T(8,128)(2,1)} %get-tuple-element.73) | copy-start | bytes 9437188
  181.8 4.0 %copy-start.24 = (bf16[768,1536]{1,0:T(8,128)(2,1)S(1)}, bf16[768,1536]{1,0:T(8,128)(2,1)}, u32[]{:S(2)}) copy-start(bf16[768,1536]{1,0:T(8,128)(2,1)} %get-tuple-element.74) | copy-start | bytes 7077892
  219.3 5.0 %copy-start.2 = (bf16[128,2176]{1,0:T(8,128)(2,1)}, bf16[128,2176]{1,0:T(8,128)(2,1)S(1)}, u32[]{:S(2)}) copy-start(bf16[128,2176]{1,0:T(8,128)(2,1)S(1)} %get-tuple-element.80.refs_0_) | copy-start | bytes 1671172
  219.3 15.6 %collective-permute-start.10 = (bf16[128,2176]{1,0:T(8,128)(2,1)S(1)}, bf16[128,2176]{1,0:T(8,128)(2,1)S(1)}, u32[]{:S(2)}, u32[]{:S(2)}) collective-permute-start(bf16[128,2176]{1,0:T(8,128)(2,1)S(1)} %get-tuple-element.80.refs_0_), channel_id=1, source_target_pairs={{0,4},{1,5},{2,6},{3,7},{4,8},{5,9},{6,10},{7,11},{8,12},{9,13},{1... | collective-permute-start | bytes 1671176 | tf_op jit(solution)/shard_map/ppermute | solution.py:616
  220.6 16.1 %collective-permute-start.13 = (bf16[128,2176]{1,0:T(8,128)(2,1)S(1)}, bf16[128,2176]{1,0:T(8,128)(2,1)S(1)}, u32[]{:S(2)}, u32[]{:S(2)}) collective-permute-start(bf16[128,2176]{1,0:T(8,128)(2,1)S(1)} %get-tuple-element.80.refs_0_), channel_id=1, source_target_pairs={{0,2},{1,3},{2,0},{3,1},{4,6},{5,7},{6,4},{7,5},{8,10},{9,11},{10,... | collective-permute-start | bytes 1671176 | tf_op jit(solution)/shard_map/ppermute | solution.py:616
  220.8 31.2 %collective-permute-start.11 = (bf16[128,2176]{1,0:T(8,128)(2,1)S(1)}, bf16[128,2176]{1,0:T(8,128)(2,1)S(1)}, u32[]{:S(2)}, u32[]{:S(2)}) collective-permute-start(bf16[128,2176]{1,0:T(8,128)(2,1)S(1)} %get-tuple-element.80.refs_0_), channel_id=1, source_target_pairs={{0,8},{1,9},{2,10},{3,11},{4,12},{5,13},{6,14},{7,15},{8,0},{9,1},... | collective-permute-start | bytes 1671176 | tf_op jit(solution)/shard_map/ppermute | solution.py:616
  224.3 27.7 %collective-permute-start.12 = (bf16[128,2176]{1,0:T(8,128)(2,1)S(1)}, bf16[128,2176]{1,0:T(8,128)(2,1)S(1)}, u32[]{:S(2)}, u32[]{:S(2)}) collective-permute-start(bf16[128,2176]{1,0:T(8,128)(2,1)S(1)} %get-tuple-element.80.refs_0_), channel_id=1, source_target_pairs={{0,12},{1,13},{2,14},{3,15},{4,0},{5,1},{6,2},{7,3},{8,4},{9,5},{1... | collective-permute-start | bytes 1671176 | tf_op jit(solution)/shard_map/ppermute | solution.py:616
  235.7 17.6 %collective-permute-start.14 = (bf16[128,768]{1,0:T(8,128)(2,1)S(1)}, bf16[128,768]{1,0:T(8,128)(2,1)S(1)}, u32[]{:S(2)}, u32[]{:S(2)}) collective-permute-start(bf16[128,768]{1,0:T(8,128)(2,1)S(1)} %slice.35), channel_id=1, source_target_pairs={{0,2},{1,3},{2,0},{3,1},{4,6},{5,7},{6,4},{7,5},{8,10},{9,11},{10,... | collective-permute-start | bytes 589832 | tf_op jit(solution)/shard_map/ppermute | solution.py:616
  236.7 15.3 %copy-start.11 = (bf16[128,2176]{1,0:T(8,128)(2,1)}, bf16[128,2176]{1,0:T(8,128)(2,1)S(1)}, u32[]{:S(2)}) copy-start(bf16[128,2176]{1,0:T(8,128)(2,1)S(1)} %collective-permute-done.13.refs_4_) | copy-start | bytes 1671172
  236.7 25.6 %collective-permute-start.17 = (bf16[128,1408]{1,0:T(8,128)(2,1)S(1)}, bf16[128,1408]{1,0:T(8,128)(2,1)}, u32[]{:S(2)}, u32[]{:S(2)}) collective-permute-start(bf16[128,1408]{1,0:T(8,128)(2,1)S(1)} %slice.38), channel_id=1, source_target_pairs={{0,4},{1,5},{2,6},{3,7},{4,8},{5,9},{6,10},{7,11},{8,12},{9,13},{1... | collective-permute-start | bytes 1081352 | tf_op jit(solution)/shard_map/ppermute | solution.py:616
  236.9 25.4 %collective-permute-start.18 = (bf16[128,1408]{1,0:T(8,128)(2,1)S(1)}, bf16[128,1408]{1,0:T(8,128)(2,1)}, u32[]{:S(2)}, u32[]{:S(2)}) collective-permute-start(bf16[128,1408]{1,0:T(8,128)(2,1)S(1)} %slice.38), channel_id=1, source_target_pairs={{0,8},{1,9},{2,10},{3,11},{4,12},{5,13},{6,14},{7,15},{8,0},{9,1},... | collective-permute-start | bytes 1081352 | tf_op jit(solution)/shard_map/ppermute | solution.py:616
  252.0 1.4 copy-start.13
  252.0 13.0 %collective-permute-start.19 = (bf16[128,1408]{1,0:T(8,128)(2,1)S(1)}, bf16[128,1408]{1,0:T(8,128)(2,1)}, u32[]{:S(2)}, u32[]{:S(2)}) collective-permute-start(bf16[128,1408]{1,0:T(8,128)(2,1)S(1)} %slice.38), channel_id=1, source_target_pairs={{0,12},{1,13},{2,14},{3,15},{4,0},{5,1},{6,2},{7,3},{8,4},{9,5},{1... | collective-permute-start | bytes 1081352 | tf_op jit(solution)/shard_map/ppermute | solution.py:616
  252.0 1.3 copy-start.14
  252.0 8.2 %collective-permute-start.15 = (bf16[128,768]{1,0:T(8,128)(2,1)S(1)}, bf16[128,768]{1,0:T(8,128)(2,1)}, u32[]{:S(2)}, u32[]{:S(2)}) collective-permute-start(bf16[128,768]{1,0:T(8,128)(2,1)S(1)} %slice.36), channel_id=1, source_target_pairs={{0,2},{1,3},{2,0},{3,1},{4,6},{5,7},{6,4},{7,5},{8,10},{9,11},{10,... | collective-permute-start | bytes 589832 | tf_op jit(solution)/shard_map/ppermute | solution.py:616
  253.4 11.6 %copy-start.15 = (bf16[128,768]{1,0:T(8,128)(2,1)}, bf16[128,768]{1,0:T(8,128)(2,1)S(1)}, u32[]{:S(2)}) copy-start(bf16[128,768]{1,0:T(8,128)(2,1)S(1)} %collective-permute-done.14.refs_5_) | copy-start | bytes 589828
  253.4 9.0 %collective-permute-start.16 = (bf16[128,768]{1,0:T(8,128)(2,1)S(1)}, bf16[128,768]{1,0:T(8,128)(2,1)}, u32[]{:S(2)}, u32[]{:S(2)}) collective-permute-start(bf16[128,768]{1,0:T(8,128)(2,1)S(1)} %slice.37), channel_id=1, source_target_pairs={{0,2},{1,3},{2,0},{3,1},{4,6},{5,7},{6,4},{7,5},{8,10},{9,11},{10,... | collective-permute-start | bytes 589832 | tf_op jit(solution)/shard_map/ppermute | solution.py:616
  265.0 48.2 %all-to-all-start.2 = ((bf16[128,8,1536]{2,1,0:T(8,128)(2,1)}), bf16[128,8,1536]{2,1,0:T(8,128)(2,1)S(1)}, u32[]{:S(2)}, u32[]{:S(2)}) async-start(bf16[128,8,1536]{2,1,0:T(8,128)(2,1)} %bitcast.50), calls=%async_computation.2 | async-start | bytes 6291456 | tf_op jit(solution)/shard_map/all_to_all | solution.py:587
  276.9 3.0 collective-permute-start.20
  277.1 2.8 collective-permute-start.21
  285.7 35.3 %collective-permute-start.22 = (bf16[2,272,256]{2,1,0:T(8,128)(2,1)}, bf16[2,272,256]{2,1,0:T(8,128)(2,1)}, u32[]{:S(2)}, u32[]{:S(2)}) collective-permute-start(bf16[2,272,256]{2,1,0:T(8,128)(2,1)} %get-tuple-element.94), channel_id=1, source_target_pairs={{0,32},{16,48},{32,64},{48,80},{64,96},{80,112},{96,0},{112,16},{1... | collective-permute-start | bytes 835592 | tf_op jit(solution)/shard_map/ppermute | solution.py:721
  287.2 33.8 %collective-permute-start.23 = (bf16[2,272,256]{2,1,0:T(8,128)(2,1)}, bf16[2,272,256]{2,1,0:T(8,128)(2,1)}, u32[]{:S(2)}, u32[]{:S(2)}) collective-permute-start(bf16[2,272,256]{2,1,0:T(8,128)(2,1)} %get-tuple-element.95), channel_id=1, source_target_pairs={{0,64},{16,80},{32,96},{48,112},{64,0},{80,16},{96,32},{112,48},{1... | collective-permute-start | bytes 835592 | tf_op jit(solution)/shard_map/ppermute | solution.py:721
  289.9 31.1 %collective-permute-start.24 = (bf16[2,272,256]{2,1,0:T(8,128)(2,1)}, bf16[2,272,256]{2,1,0:T(8,128)(2,1)}, u32[]{:S(2)}, u32[]{:S(2)}) collective-permute-start(bf16[2,272,256]{2,1,0:T(8,128)(2,1)} %get-tuple-element.96), channel_id=1, source_target_pairs={{0,96},{16,112},{32,0},{48,16},{64,32},{80,48},{96,64},{112,80},{1... | collective-permute-start | bytes 835592 | tf_op jit(solution)/shard_map/ppermute | solution.py:721
  297.5 26.9 %collective-permute-start.25 = (bf16[8,128,256]{2,1,0:T(8,128)(2,1)}, bf16[8,128,256]{2,1,0:T(8,128)(2,1)}, u32[]{:S(2)}, u32[]{:S(2)}) collective-permute-start(bf16[8,128,256]{2,1,0:T(8,128)(2,1)} %get-tuple-element.99), channel_id=1, source_target_pairs={{0,1},{1,0},{2,3},{3,2},{4,5},{5,4},{6,7},{7,6},{8,9},{9,8},{10,11... | collective-permute-start | bytes 1572872 | tf_op jit(solution)/shard_map/ppermute | solution.py:616
  314.3 6.8 %copy-start.16 = (bf16[2,272,256]{2,1,0:T(8,128)(2,1)S(1)}, bf16[2,272,256]{2,1,0:T(8,128)(2,1)}, u32[]{:S(2)}) copy-start(bf16[2,272,256]{2,1,0:T(8,128)(2,1)} %get-tuple-element.101) | copy-start | bytes 835588
  322.3 5.6 %collective-permute-start.26 = (bf16[272,256]{1,0:T(8,128)(2,1)S(1)}, bf16[272,256]{1,0:T(8,128)(2,1)S(1)}, u32[]{:S(2)}, u32[]{:S(2)}) collective-permute-start(bf16[272,256]{1,0:T(8,128)(2,1)S(1)} %fusion.3), channel_id=1, source_target_pairs={{0,16},{16,0},{32,48},{48,32},{64,80},{80,64},{96,112},{112,96},{1... | collective-permute-start | bytes 417800 | tf_op jit(solution)/shard_map/ppermute | solution.py:726
  (6 other events, 5.8 us)
